TPU v7x, 512 devices: a whole 4x8x8 slice. The times are simulated.
512 devices in a mesh: wide: 32 (over x, z), narrow: 16 (over y, core).
Axes of the slice: x: 4, y: 8, z: 8, core: 2. Of those that a mesh axis runs over, the one named last changes fastest.
Arguments:
- embeddings: bfloat16 [131072, 1024], P(('wide', 'narrow')), may hold values from -40 to 40
- labels: int32 [131072], P(('wide', 'narrow')), may hold values from 0 to 127, as said below
Outputs:
- nearest: float32 [131072], P(('wide', 'narrow'))
Inputs may be any that keep to these rules, and one draw needn't show every extreme that they name: In each aligned block of 256 rows (one device's documents), at most 16 labels lie in any one range of 4 consecutive cluster numbers starting at a multiple of 4, and exactly 16 in some such range.
All inputs are finite; a program needn't handle non-finite values.
Results may differ from a plain program's by a relative error of at most 0.00049.
Values may be sent and summed in bfloat16 or wider, within the bound.
No kernel may reach another device: no remote copies, remote signals or barrier semaphores. Data moves between devices by JAX's collectives and lax.ppermute only.
A program may use at most 64 MiB of HBM per device.

v0:
```python
import math

import jax
import jax.numpy as jnp
from jax import lax
from jax.sharding import PartitionSpec as P

CL_GROUP = 4


def masked_scores(left, left_labels, right, right_labels):
    scores = lax.dot_general(
        left, right, (((1,), (1,)), ((), ())), preferred_element_type=jnp.float32
    )
    allowed = (left_labels[:, None] == right_labels[None, :]) & (left_labels[:, None] >= 0)
    return jnp.where(allowed, scores, jnp.float32(-1.0))


def fold_piece(best, rows, row_labels, own_index, piece_rows, piece_labels):
    amount = piece_rows.shape[0]
    stride = 512

    def advance(carry, position):
        first = position * stride
        portion = lax.dynamic_slice_in_dim(piece_rows, first, stride, 0)
        portion_labels = lax.dynamic_slice_in_dim(piece_labels, first, stride, 0)
        scores = masked_scores(rows, row_labels, portion, portion_labels)
        column = first + jnp.arange(stride, dtype=jnp.int32)
        scores = jnp.where(own_index[:, None] == column[None, :], jnp.float32(-1.0), scores)
        return (jnp.maximum(carry, jnp.max(scores, axis=1)), None)

    best, unused = lax.scan(advance, best, jnp.arange(amount // stride, dtype=jnp.int32))
    return best


def shards(embeddings, labels):
    doc_count, width = embeddings.shape
    groups_count = lax.axis_size("wide")
    capacity = 2 * doc_count // groups_count
    values = embeddings.astype(jnp.float32)
    unit = (
        values
        * lax.rsqrt(jnp.mean(values * values, axis=1, keepdims=True) + 1e-06)
        / math.sqrt(width)
    ).astype(jnp.bfloat16)
    owner = labels // CL_GROUP
    onehot = (owner[:, None] == jnp.arange(groups_count, dtype=jnp.int32)[None, :]).astype(
        jnp.int32
    )
    ranked = jnp.sum(jnp.cumsum(onehot, axis=0) * onehot, axis=1) - 1
    placed = owner * capacity + ranked
    outgoing = jnp.zeros((groups_count * capacity, width), jnp.bfloat16).at[placed].set(unit)
    outgoing_labels = jnp.full((groups_count * capacity,), -1, jnp.int32).at[placed].set(labels)
    rows, row_labels = (
        lax.all_to_all(outgoing, "wide", split_axis=0, concat_axis=0, tiled=True),
        lax.all_to_all(outgoing_labels, "wide", split_axis=0, concat_axis=0, tiled=True),
    )
    slots_count = rows.shape[0]
    floor_values = jnp.full((slots_count,), -1.0, jnp.float32)
    local_index = jnp.arange(slots_count, dtype=jnp.int32)
    own_index = lax.axis_index("narrow") * slots_count + local_index
    best = fold_piece(
        floor_values,
        rows,
        row_labels,
        own_index,
        lax.all_gather(rows, "narrow", axis=0, tiled=True),
        lax.all_gather(row_labels, "narrow", axis=0, tiled=True),
    )
    answers = lax.all_to_all(best, "wide", split_axis=0, concat_axis=0, tiled=True)
    return answers[placed]


def solution(mesh):
    in_specs = (P(("wide", "narrow"), None), P(("wide", "narrow")))
    out_specs = P(("wide", "narrow"))
    return jax.shard_map(shards, mesh=mesh, in_specs=in_specs, out_specs=out_specs, check_vma=False)
```

profile of v0, /device:TPU:1, one launch (start us, length us, event | category | flops | bytes accessed | tf_op | source)
XLA Modules:
  0.0 240.0 jit_solution(13316222575272074669)
XLA Ops:
  6.5 0.7 and_select_fusion
  7.2 0.7 fusion.21
  8.8 0.7 compare_select_fusion
  9.5 1.2 fusion.7
  10.8 2.5 %scatter_custom_fusion.1 = bf16[512,1024]{1,0:T(8,128)(2,1)S(1)} fusion(s32[256]{0:T(256)S(1)} %compare_select_fusion, bf16[256,1024]{1,0:T(8,128)(2,1)} %param.4, f32[]{:T(128)} %constant.62.clone.1, f32[256]{0:T(256)S(1)} %add_rsqrt_fusion, bf16[]{:T(256)} %constant.26.clone.1), kind=kCustom, calls=%fused_computation.19 | custom fusion | flops 1048576 | bytes 1573894 | tf_op jit(solution)/shard_map/scatter | solution.py:52
  13.3 38.2 %all_to_all.36 = bf16[32,16,1024]{2,1,0:T(8,128)(2,1)} all-to-all(bf16[32,16,1024]{2,1,0:T(8,128)(2,1)S(1)} %bitcast.43), channel_id=1, replica_groups=mesh['wide'=32,'narrow'=16] {'wide'}, dimensions={0} | all-to-all | bytes 2097152 | tf_op jit(solution)/shard_map/all_to_all | solution.py:55
  51.6 1.6 scatter_custom_fusion
  53.8 8.6 %all-to-all-start = ((s32[32,16,1]{1,2,0:T(1,128)}), s32[32,16,1]{1,2,0:T(1,128)S(1)}, u32[]{:S(2)}, u32[]{:S(2)}) async-start(s32[32,16,1]{1,2,0:T(1,128)} %bitcast.2), calls=%async_computation | async-start | bytes 32768 | tf_op jit(solution)/shard_map/all_to_all | solution.py:56
  62.4 8.6 %all-to-all-done = s32[32,16,1]{1,2,0:T(1,128)S(1)} async-done(((s32[32,16,1]{1,2,0:T(1,128)}), s32[32,16,1]{1,2,0:T(1,128)S(1)}, u32[]{:S(2)}, u32[]{:S(2)}) %all-to-all-start) | async-done | bytes 2080 | tf_op jit(solution)/shard_map/all_to_all | solution.py:56
  72.3 20.1 %all-gather = s32[16,1,512]{2,1,0:T(1,128)S(1)} all-gather(s32[1,1,512]{2,1,0:T(1,128)S(1)} %reshape.71), channel_id=1, replica_groups=mesh['wide'=32,'narrow'=16] {'narrow'}, dimensions={0}, use_global_device_ids=true | all-gather | bytes 34816 | tf_op jit(solution)/shard_map/all_gather | solution.py:68
  92.4 58.5 %all-gather.3.cloned.1.call-done = bf16[8192,1024]{1,0:T(8,128)(2,1)} async-done(((bf16[512,1024]{1,0:T(8,128)(2,1)}), bf16[8192,1024]{1,0:T(8,128)(2,1)}) %all-gather.3.cloned.1.call-update) | async-done | bytes 16777232 | tf_op jit(solution)/shard_map/all_gather | solution.py:67
  150.9 59.3 %while.11 = (s32[]{:T(128)}, f32[512]{0:T(512)S(1)}, s32[16]{0:T(128)S(1)}, s32[512]{0:T(512)S(1)}, s32[8192]{0:T(1024)S(1)}, /*index=5*/bf16[8192,1024]{1,0:T(8...) while((s32[]{:T(128)}, f32[512]{0:T(512)S(1)}, ...), condition=%wide.region_8.9_spmd.clone, body=%wide.region_6.8_spmd.clone.sunk | while | flops 538445824 | bytes 2125009 | solution.py:32
  152.2 2.4 %fusion.27 = f32[512]{0:T(512)S(1)} fusion(bf16[512,1024]{1,0:T(8,128)(2,1)} %get-tuple-element.179, bf16[8192,1024]{1,0:T(8,128)(2,1)} %get-tuple-element.178, s32[]{:T(128)S(6)} %select_n.46, s32[512]{0:T(512)S(1)} %get-tuple-element.176, s32[512]{0:T(512)S(1)} %get-tuple-element.147, s32[512]{0:T(512)S(1)} %dynamic_slice.20, ...), kind=kOutput, calls=%fused_computation.7.clone.1 | convolution fusion | flops 538443264 | bytes 2107908 | tf_op jit(solution)/shard_map/while/body/eval_jaxpr/dot_general | solution.py:12
  155.9 2.4 %fusion.27 = f32[512]{0:T(512)S(1)} fusion(bf16[512,1024]{1,0:T(8,128)(2,1)} %get-tuple-element.179, bf16[8192,1024]{1,0:T(8,128)(2,1)} %get-tuple-element.178, s32[]{:T(128)S(6)} %select_n.46, s32[512]{0:T(512)S(1)} %get-tuple-element.176, s32[512]{0:T(512)S(1)} %get-tuple-element.147, s32[512]{0:T(512)S(1)} %dynamic_slice.20, ...), kind=kOutput, calls=%fused_computation.7.clone.1 | convolution fusion | flops 538443264 | bytes 2107908 | tf_op jit(solution)/shard_map/while/body/eval_jaxpr/dot_general | solution.py:12
  159.6 2.4 %fusion.27 = f32[512]{0:T(512)S(1)} fusion(bf16[512,1024]{1,0:T(8,128)(2,1)} %get-tuple-element.179, bf16[8192,1024]{1,0:T(8,128)(2,1)} %get-tuple-element.178, s32[]{:T(128)S(6)} %select_n.46, s32[512]{0:T(512)S(1)} %get-tuple-element.176, s32[512]{0:T(512)S(1)} %get-tuple-element.147, s32[512]{0:T(512)S(1)} %dynamic_slice.20, ...), kind=kOutput, calls=%fused_computation.7.clone.1 | convolution fusion | flops 538443264 | bytes 2107908 | tf_op jit(solution)/shard_map/while/body/eval_jaxpr/dot_general | solution.py:12
  163.3 2.4 %fusion.27 = f32[512]{0:T(512)S(1)} fusion(bf16[512,1024]{1,0:T(8,128)(2,1)} %get-tuple-element.179, bf16[8192,1024]{1,0:T(8,128)(2,1)} %get-tuple-element.178, s32[]{:T(128)S(6)} %select_n.46, s32[512]{0:T(512)S(1)} %get-tuple-element.176, s32[512]{0:T(512)S(1)} %get-tuple-element.147, s32[512]{0:T(512)S(1)} %dynamic_slice.20, ...), kind=kOutput, calls=%fused_computation.7.clone.1 | convolution fusion | flops 538443264 | bytes 2107908 | tf_op jit(solution)/shard_map/while/body/eval_jaxpr/dot_general | solution.py:12
  167.0 2.4 %fusion.27 = f32[512]{0:T(512)S(1)} fusion(bf16[512,1024]{1,0:T(8,128)(2,1)} %get-tuple-element.179, bf16[8192,1024]{1,0:T(8,128)(2,1)} %get-tuple-element.178, s32[]{:T(128)S(6)} %select_n.46, s32[512]{0:T(512)S(1)} %get-tuple-element.176, s32[512]{0:T(512)S(1)} %get-tuple-element.147, s32[512]{0:T(512)S(1)} %dynamic_slice.20, ...), kind=kOutput, calls=%fused_computation.7.clone.1 | convolution fusion | flops 538443264 | bytes 2107908 | tf_op jit(solution)/shard_map/while/body/eval_jaxpr/dot_general | solution.py:12
  170.7 2.4 %fusion.27 = f32[512]{0:T(512)S(1)} fusion(bf16[512,1024]{1,0:T(8,128)(2,1)} %get-tuple-element.179, bf16[8192,1024]{1,0:T(8,128)(2,1)} %get-tuple-element.178, s32[]{:T(128)S(6)} %select_n.46, s32[512]{0:T(512)S(1)} %get-tuple-element.176, s32[512]{0:T(512)S(1)} %get-tuple-element.147, s32[512]{0:T(512)S(1)} %dynamic_slice.20, ...), kind=kOutput, calls=%fused_computation.7.clone.1 | convolution fusion | flops 538443264 | bytes 2107908 | tf_op jit(solution)/shard_map/while/body/eval_jaxpr/dot_general | solution.py:12
  174.4 2.4 %fusion.27 = f32[512]{0:T(512)S(1)} fusion(bf16[512,1024]{1,0:T(8,128)(2,1)} %get-tuple-element.179, bf16[8192,1024]{1,0:T(8,128)(2,1)} %get-tuple-element.178, s32[]{:T(128)S(6)} %select_n.46, s32[512]{0:T(512)S(1)} %get-tuple-element.176, s32[512]{0:T(512)S(1)} %get-tuple-element.147, s32[512]{0:T(512)S(1)} %dynamic_slice.20, ...), kind=kOutput, calls=%fused_computation.7.clone.1 | convolution fusion | flops 538443264 | bytes 2107908 | tf_op jit(solution)/shard_map/while/body/eval_jaxpr/dot_general | solution.py:12
  178.1 2.4 %fusion.27 = f32[512]{0:T(512)S(1)} fusion(bf16[512,1024]{1,0:T(8,128)(2,1)} %get-tuple-element.179, bf16[8192,1024]{1,0:T(8,128)(2,1)} %get-tuple-element.178, s32[]{:T(128)S(6)} %select_n.46, s32[512]{0:T(512)S(1)} %get-tuple-element.176, s32[512]{0:T(512)S(1)} %get-tuple-element.147, s32[512]{0:T(512)S(1)} %dynamic_slice.20, ...), kind=kOutput, calls=%fused_computation.7.clone.1 | convolution fusion | flops 538443264 | bytes 2107908 | tf_op jit(solution)/shard_map/while/body/eval_jaxpr/dot_general | solution.py:12
  181.8 2.4 %fusion.27 = f32[512]{0:T(512)S(1)} fusion(bf16[512,1024]{1,0:T(8,128)(2,1)} %get-tuple-element.179, bf16[8192,1024]{1,0:T(8,128)(2,1)} %get-tuple-element.178, s32[]{:T(128)S(6)} %select_n.46, s32[512]{0:T(512)S(1)} %get-tuple-element.176, s32[512]{0:T(512)S(1)} %get-tuple-element.147, s32[512]{0:T(512)S(1)} %dynamic_slice.20, ...), kind=kOutput, calls=%fused_computation.7.clone.1 | convolution fusion | flops 538443264 | bytes 2107908 | tf_op jit(solution)/shard_map/while/body/eval_jaxpr/dot_general | solution.py:12
  185.5 2.4 %fusion.27 = f32[512]{0:T(512)S(1)} fusion(bf16[512,1024]{1,0:T(8,128)(2,1)} %get-tuple-element.179, bf16[8192,1024]{1,0:T(8,128)(2,1)} %get-tuple-element.178, s32[]{:T(128)S(6)} %select_n.46, s32[512]{0:T(512)S(1)} %get-tuple-element.176, s32[512]{0:T(512)S(1)} %get-tuple-element.147, s32[512]{0:T(512)S(1)} %dynamic_slice.20, ...), kind=kOutput, calls=%fused_computation.7.clone.1 | convolution fusion | flops 538443264 | bytes 2107908 | tf_op jit(solution)/shard_map/while/body/eval_jaxpr/dot_general | solution.py:12
  189.2 2.4 %fusion.27 = f32[512]{0:T(512)S(1)} fusion(bf16[512,1024]{1,0:T(8,128)(2,1)} %get-tuple-element.179, bf16[8192,1024]{1,0:T(8,128)(2,1)} %get-tuple-element.178, s32[]{:T(128)S(6)} %select_n.46, s32[512]{0:T(512)S(1)} %get-tuple-element.176, s32[512]{0:T(512)S(1)} %get-tuple-element.147, s32[512]{0:T(512)S(1)} %dynamic_slice.20, ...), kind=kOutput, calls=%fused_computation.7.clone.1 | convolution fusion | flops 538443264 | bytes 2107908 | tf_op jit(solution)/shard_map/while/body/eval_jaxpr/dot_general | solution.py:12
  192.9 2.4 %fusion.27 = f32[512]{0:T(512)S(1)} fusion(bf16[512,1024]{1,0:T(8,128)(2,1)} %get-tuple-element.179, bf16[8192,1024]{1,0:T(8,128)(2,1)} %get-tuple-element.178, s32[]{:T(128)S(6)} %select_n.46, s32[512]{0:T(512)S(1)} %get-tuple-element.176, s32[512]{0:T(512)S(1)} %get-tuple-element.147, s32[512]{0:T(512)S(1)} %dynamic_slice.20, ...), kind=kOutput, calls=%fused_computation.7.clone.1 | convolution fusion | flops 538443264 | bytes 2107908 | tf_op jit(solution)/shard_map/while/body/eval_jaxpr/dot_general | solution.py:12
  196.6 2.4 %fusion.27 = f32[512]{0:T(512)S(1)} fusion(bf16[512,1024]{1,0:T(8,128)(2,1)} %get-tuple-element.179, bf16[8192,1024]{1,0:T(8,128)(2,1)} %get-tuple-element.178, s32[]{:T(128)S(6)} %select_n.46, s32[512]{0:T(512)S(1)} %get-tuple-element.176, s32[512]{0:T(512)S(1)} %get-tuple-element.147, s32[512]{0:T(512)S(1)} %dynamic_slice.20, ...), kind=kOutput, calls=%fused_computation.7.clone.1 | convolution fusion | flops 538443264 | bytes 2107908 | tf_op jit(solution)/shard_map/while/body/eval_jaxpr/dot_general | solution.py:12
  200.3 2.4 %fusion.27 = f32[512]{0:T(512)S(1)} fusion(bf16[512,1024]{1,0:T(8,128)(2,1)} %get-tuple-element.179, bf16[8192,1024]{1,0:T(8,128)(2,1)} %get-tuple-element.178, s32[]{:T(128)S(6)} %select_n.46, s32[512]{0:T(512)S(1)} %get-tuple-element.176, s32[512]{0:T(512)S(1)} %get-tuple-element.147, s32[512]{0:T(512)S(1)} %dynamic_slice.20, ...), kind=kOutput, calls=%fused_computation.7.clone.1 | convolution fusion | flops 538443264 | bytes 2107908 | tf_op jit(solution)/shard_map/while/body/eval_jaxpr/dot_general | solution.py:12
  204.0 2.4 %fusion.27 = f32[512]{0:T(512)S(1)} fusion(bf16[512,1024]{1,0:T(8,128)(2,1)} %get-tuple-element.179, bf16[8192,1024]{1,0:T(8,128)(2,1)} %get-tuple-element.178, s32[]{:T(128)S(6)} %select_n.46, s32[512]{0:T(512)S(1)} %get-tuple-element.176, s32[512]{0:T(512)S(1)} %get-tuple-element.147, s32[512]{0:T(512)S(1)} %dynamic_slice.20, ...), kind=kOutput, calls=%fused_computation.7.clone.1 | convolution fusion | flops 538443264 | bytes 2107908 | tf_op jit(solution)/shard_map/while/body/eval_jaxpr/dot_general | solution.py:12
  207.7 2.4 %fusion.27 = f32[512]{0:T(512)S(1)} fusion(bf16[512,1024]{1,0:T(8,128)(2,1)} %get-tuple-element.179, bf16[8192,1024]{1,0:T(8,128)(2,1)} %get-tuple-element.178, s32[]{:T(128)S(6)} %select_n.46, s32[512]{0:T(512)S(1)} %get-tuple-element.176, s32[512]{0:T(512)S(1)} %get-tuple-element.147, s32[512]{0:T(512)S(1)} %dynamic_slice.20, ...), kind=kOutput, calls=%fused_computation.7.clone.1 | convolution fusion | flops 538443264 | bytes 2107908 | tf_op jit(solution)/shard_map/while/body/eval_jaxpr/dot_general | solution.py:12
  210.9 9.9 %all-to-all-start.2 = ((f32[32,16,1]{1,2,0:T(1,128)}), f32[32,16,1]{1,2,0:T(1,128)S(1)}, u32[]{:S(2)}, u32[]{:S(2)}) async-start(f32[32,16,1]{1,2,0:T(1,128)} %bitcast.6), calls=%async_computation.2 | async-start | bytes 32768 | tf_op jit(solution)/shard_map/all_to_all | solution.py:70
  220.8 8.6 %all-to-all-done.2 = f32[32,16,1]{1,2,0:T(1,128)S(1)} async-done(((f32[32,16,1]{1,2,0:T(1,128)}), f32[32,16,1]{1,2,0:T(1,128)S(1)}, u32[]{:S(2)}, u32[]{:S(2)}) %all-to-all-start.2) | async-done | bytes 2080 | tf_op jit(solution)/shard_map/all_to_all | solution.py:70
  229.9 0.7 reduce.11
  230.7 2.5 %gather_fusion = f32[256]{0:T(256)} fusion(f32[512]{0:T(512)S(1)} %all_to_all.32, s32[1024]{0:T(1024)S(1)} %pad_clamp_fusion), kind=kCustom, calls=%fused_computation | custom fusion | bytes 3072 | tf_op jit(solution)/shard_map/gather | solution.py:71
  (100 shorter events, 15.3 us)
Async XLA Ops:
  6.5 144.4 %all-gather.3.cloned.1.call-start = ((), (), s32[]{:S(2)}) async-start(), calls=%async_computation.3 | async-start | bytes 17825792 | tf_op jit(solution)/shard_map/all_gather | solution.py:67
  53.8 17.2 %all-to-all-start = ((s32[32,16,1]{1,2,0:T(1,128)}), s32[32,16,1]{1,2,0:T(1,128)S(1)}, u32[]{:S(2)}, u32[]{:S(2)}) async-start(s32[32,16,1]{1,2,0:T(1,128)} %bitcast.2), calls=%async_computation | async-start | bytes 32768 | tf_op jit(solution)/shard_map/all_to_all | solution.py:56
  210.9 18.5 %all-to-all-start.2 = ((f32[32,16,1]{1,2,0:T(1,128)}), f32[32,16,1]{1,2,0:T(1,128)S(1)}, u32[]{:S(2)}, u32[]{:S(2)}) async-start(f32[32,16,1]{1,2,0:T(1,128)} %bitcast.6), calls=%async_computation.2 | async-start | bytes 32768 | tf_op jit(solution)/shard_map/all_to_all | solution.py:70
Sparse Core Ops, SparseCore 0:
  51.7 99.1 all-gather.2
where the time goes:
time: 241 us; the launch traced here: 240 us
  waiting for transfers between devices  75.7 us (31%)
  blocking collectives  58.4 us (24%)
  matrix products  38.5 us (16%)
  starting transfers between devices  18.5 us (8%)
  local copies, waits for them, and re-layouts  17.6 us (7%)
  between operations  13.5 us (6%)
  loops' own time  9.68 us (4%)
  other arithmetic  8.24 us (3%)
    all_gather x1, waiting for transfers between devices, shards(): lax.all_gather(rows, 'narrow', axis=0, tiled=True)  58.5 us
    dot_general x16, matrix products, masked_scores(): lax.dot_general(left, right, (((1,), (1,)), ((), ())), preferred_element_...  38.5 us
    all_to_all x1, blocking collectives, shards(): lax.all_to_all(outgoing, 'wide', split_axis=0, concat_axis=0, tiled=True)  38.2 us
    all_gather x1, blocking collectives, shards(): lax.all_gather(row_labels, 'narrow', axis=0, tiled=True)  20.1 us
    all_to_all x1, starting transfers between devices, shards(): lax.all_to_all(best, 'wide', split_axis=0, concat_axis=0, tiled=True)  9.9 us
    another operation x1, loops' own time, fold_piece(): lax.scan(advance, best, jnp.arange(amount // stride, dtype=jnp.int32))  9.68 us
    dynamic_slice x16, local copies, waits for them, and re-layouts, fold_piece(): lax.scan(advance, best, jnp.arange(amount // stride, dtype=jnp.int32))  9.42 us
    all_to_all x1, waiting for transfers between devices, shards(): lax.all_to_all(outgoing_labels, 'wide', split_axis=0, concat_axis=0, tile...  8.62 us
  transfers between devices with their start and end apart: 3, of which 3 were waited for; matrix products, arithmetic and copies ran while one was open for 1% of the time, Pallas kernels for 0%

commit v1 on v0

v1 whole, which is shorter than its diff:
```python
import functools
import math

import jax
import jax.numpy as jnp
from jax import lax
from jax.experimental import pallas as pl
from jax.experimental.pallas import tpu as pltpu
from jax.sharding import PartitionSpec as P

CL_GROUP = 4
CAP = 16
LIFT = 4.0
LABEL_ROWS = 16
F32, BF16, I32 = jnp.float32, jnp.bfloat16, jnp.int32
NT = (((1,), (1,)), ((), ()))
NN = (((1,), (0,)), ((), ()))
TN = (((0,), (0,)), ((), ()))
VMEM = pl.BlockSpec(memory_space=pltpu.VMEM)
SMEM = pl.BlockSpec(memory_space=pltpu.SMEM)


def dot(a, b, dims):
    return lax.dot_general(a, b, dims, preferred_element_type=F32)


def iota(shape, dim):
    return lax.broadcasted_iota(I32, shape, dim)


def one_hot(condition):
    return condition.astype(F32).astype(BF16)


def call(kernel, out_shape, in_specs, flops, size):
    return pl.pallas_call(
        kernel,
        out_shape=out_shape,
        in_specs=in_specs,
        out_specs=jax.tree.map(lambda _: VMEM, out_shape),
        compiler_params=pltpu.CompilerParams(vmem_limit_bytes=40 * 1024 * 1024),
        cost_estimate=pl.CostEstimate(flops=flops, bytes_accessed=size, transcendentals=0),
    )


def place_kernel(offset_ref, rows_ref, labels_ref, out_ref, slot_ref):
    docs, width = rows_ref.shape
    groups, tall, lanes = out_ref.shape
    labels = labels_ref[...]
    owner = labels >> 2
    mine = iota((groups, docs), 0) == owner
    before = one_hot(iota((docs, docs), 0) < iota((docs, docs), 1))
    earlier = dot(one_hot(mine), before, NN)
    rank = jnp.sum(jnp.where(mine, earlier, 0.0), axis=0, keepdims=True).astype(I32)
    slot = owner * CAP + rank
    slot_ref[...] = slot
    values = rows_ref[...].astype(F32)
    mean = jnp.mean(values * values, axis=1, keepdims=True)
    unit = (values * lax.rsqrt(mean + 1e-06) / math.sqrt(width)).astype(BF16)
    pick = one_hot(iota((groups * CAP, docs), 0) == slot)
    step = 2 * lanes
    for first in range(0, width, step):
        placed = dot(pick, unit[:, first : first + step], NN).astype(BF16)
        for half in range(2):
            k = first // lanes + half
            part = placed[:, half * lanes : (half + 1) * lanes]
            out_ref[:, k * CAP : (k + 1) * CAP, :] = part.reshape(groups, CAP, lanes)
    below = tall - CAP * width // lanes
    index = iota((groups * below, docs), 0)
    cluster = index & (below - 1)
    wanted = (labels == (index >> 3) * CL_GROUP + cluster) & (cluster < CL_GROUP)
    lane = one_hot(iota((lanes, docs), 0) == rank + offset_ref[0])
    flags = dot(one_hot(wanted), lane, NT).astype(BF16)
    out_ref[:, tall - below :, :] = flags.reshape(groups, below, lanes)


def compact_kernel(capacity, in_ref, out_ref, position_ref, over_ref):
    groups, tall, lanes = in_ref.shape
    width = out_ref.shape[1]
    count = width // lanes
    slots = groups * CAP
    below = tall - CAP * count
    labels = in_ref[:, tall - below :, :].astype(F32)
    per = lanes // CAP
    labels = jnp.sum(labels.reshape(groups // per, per, below, lanes), axis=1)
    labels = jnp.concatenate([labels[i] for i in range(groups // per)], axis=1)
    valid = jnp.sum(labels, axis=0, keepdims=True)
    before = one_hot(iota((slots, slots), 0) < iota((slots, slots), 1))
    rank = dot(jnp.broadcast_to(valid, (8, slots)).astype(BF16), before, NN)[:1]
    position = jnp.where(valid > 0.5, rank.astype(I32), -1)
    position_ref[...] = position
    total = jnp.sum(valid, axis=1, keepdims=True)
    over_ref[...] = jnp.broadcast_to(jnp.where(total > capacity + 0.5, 1.0, 0.0), over_ref.shape)
    pick = one_hot(iota((capacity, slots), 0) == position)
    for k in range(count):
        part = in_ref[:, k * CAP : (k + 1) * CAP, :].reshape(slots, lanes)
        out_ref[:capacity, k * lanes : (k + 1) * lanes] = dot(pick, part, NN).astype(BF16)
    marks = dot(labels.astype(BF16), pick, NT).astype(BF16)
    marks = jnp.concatenate([marks, jnp.zeros((below, width - capacity), BF16)], axis=1)
    marks = jnp.concatenate([marks, jnp.zeros((LABEL_ROWS - below, width), BF16)], axis=0)
    out_ref[capacity:, :] = marks


def lifted(left_ref, right_ref, capacity):
    left, right = left_ref[:capacity, :], right_ref[:capacity, :]
    left_marks = left_ref[capacity:, :capacity]
    right_marks = (right_ref[capacity:, :capacity].astype(F32) * LIFT).astype(BF16)
    return dot(left, right, NT) + dot(left_marks, right_marks, TN)


def over_rows(scores):
    return jnp.max(scores, axis=0, keepdims=True)


def over_columns(scores):
    return jnp.max(scores, axis=1, keepdims=True)


def as_row(column):
    size = column.shape[0]
    same = iota((size, size), 0) == iota((size, size), 1)
    return jnp.max(jnp.where(same, column, -9.0), axis=0, keepdims=True)


def own_kernel(capacity, own_ref, twin_ref, out_ref):
    scores = lifted(own_ref, own_ref, capacity)
    same = iota((capacity, capacity), 0) == iota((capacity, capacity), 1)
    best = over_rows(jnp.where(same, -9.0, scores))
    out_ref[...] = jnp.maximum(best, over_rows(lifted(twin_ref, own_ref, capacity)))


def next_kernel(capacity, best_ref, own_ref, twin_ref, next_ref, own_out, twin_out, next_out):
    first = lifted(next_ref, own_ref, capacity)
    own_out[...] = jnp.maximum(best_ref[...], over_rows(first))
    second = lifted(next_ref, twin_ref, capacity)
    twin_out[...] = over_rows(second)
    next_out[...] = as_row(jnp.maximum(over_columns(first), over_columns(second)))


def last_kernel(
    capacity, targets_ref, over_ref, own_best, twin_best, next_best, own_ref, twin_ref,
    back_ref, back_twin_ref, far_ref, ahead_ref, out_ref,
):
    bests = []
    across = None
    for ref in (own_ref, twin_ref, back_ref, back_twin_ref, far_ref):
        scores = lifted(ahead_ref, ref, capacity)
        bests.append(over_rows(scores))
        column = over_columns(scores)
        across = column if across is None else jnp.maximum(across, column)
    bests[0] = jnp.maximum(bests[0], own_best[...])
    bests[1] = jnp.maximum(bests[1], twin_best[...])
    bests += [next_best[...], as_row(across)]
    count, wide = out_ref.shape
    rest = wide - capacity
    row = iota((count, capacity), 0)
    out = jnp.full((count, capacity), -9.0, F32)
    for i, best in enumerate(bests):
        out = jnp.where(row == targets_ref[i], best, out)
    over = jnp.broadcast_to(over_ref[...][:, :1], (count, rest))
    out_ref[...] = jnp.concatenate([out, over], axis=1)


def answer_kernel(capacity, all_ref, position_ref, out_ref):
    slots = position_ref.shape[1]
    groups, lanes = out_ref.shape
    best = jnp.max(all_ref[...], axis=0, keepdims=True)
    over = best[:, capacity : capacity + 1]
    best = jnp.maximum(best[:, :capacity] - LIFT, -1.0)
    diagonal = iota((slots, slots), 0) == iota((slots, slots), 1)
    position = jnp.max(jnp.where(diagonal, position_ref[...], -1), axis=1, keepdims=True)
    hit = iota((slots, capacity), 1) == position
    values = jnp.max(jnp.where(hit, best, -1.0), axis=1, keepdims=True)
    values = jnp.broadcast_to(values, (slots, lanes)).reshape(groups, CAP, lanes)
    same = iota((groups, CAP, lanes), 1) == iota((groups, CAP, lanes), 2)
    answers = jnp.max(jnp.where(same, values, -1.0), axis=1)
    out_ref[...] = jnp.where(iota((groups, lanes), 1) == CAP, over, answers)


def home_kernel(slot_ref, answers_ref, out_ref, over_ref):
    groups, lanes = answers_ref.shape
    docs = slot_ref.shape[1]
    answers = answers_ref[...]
    over = jnp.max(answers[:, CAP : CAP + 1], axis=0, keepdims=True)
    over_ref[...] = jnp.broadcast_to((over > 0.5).astype(I32), over_ref.shape)
    spread = jnp.broadcast_to(answers[:, None, :], (groups, CAP, lanes))
    same = iota((groups, CAP, lanes), 1) == iota((groups, CAP, lanes), 2)
    column = jnp.max(jnp.where(same, spread, -1.0), axis=2, keepdims=True)
    column = column.reshape(groups * CAP, 1)
    hit = iota((groups * CAP, docs), 0) == slot_ref[...]
    out_ref[...] = jnp.max(jnp.where(hit, column, -1.0), axis=0, keepdims=True)


def ring(step):
    size = lax.axis_size("narrow")
    return [(i, (i + 2 * step) % size) for i in range(size)]


def crossing():
    size = lax.axis_size("narrow")
    pairs = []
    for i in range(size):
        to = (i + 2) % size
        pairs.append((i, to ^ 1 if to >= size // 2 else to))
    return pairs


def nearest(received, slot, capacity):
    width = 1024
    groups, tall, lanes = received.shape
    slots = groups * CAP
    size = lax.axis_size("narrow")
    shape = jax.ShapeDtypeStruct
    block_bytes = 2 * (capacity + LABEL_ROWS) * width
    product = 2 * capacity * capacity * (width + 128)
    line = shape((1, capacity), F32)
    block, position, over = call(
        functools.partial(compact_kernel, capacity),
        (
            shape((capacity + LABEL_ROWS, width), BF16),
            shape((1, slots), I32),
            shape((1, 128), F32),
        ),
        [VMEM],
        2 * capacity * slots * width,
        received.size * 2 + block_bytes,
    )(received)

    twins = [(i, i ^ 1) for i in range(size)]
    back = lax.ppermute(block, "narrow", ring(1))
    ahead = lax.ppermute(block, "narrow", ring(-1))
    twin = lax.ppermute(block, "narrow", twins)
    far = lax.ppermute(back, "narrow", crossing())
    far_ahead = lax.ppermute(ahead, "narrow", ring(-1))
    back_twin = lax.ppermute(back, "narrow", twins)

    best = call(
        functools.partial(own_kernel, capacity), line, [VMEM] * 2, 2 * product, 2 * block_bytes
    )(block, twin)
    own_best, twin_best, next_best = call(
        functools.partial(next_kernel, capacity),
        (line, line, line),
        [VMEM] * 4,
        2 * product,
        3 * block_bytes,
    )(best, block, twin, ahead)

    me = lax.axis_index("narrow")
    crossed = jnp.where(me >= size // 2, 1, 0)
    targets = jnp.stack(
        [
            me,
            me ^ 1,
            (me - 2) % size,
            ((me - 2) % size) ^ 1,
            ((me - 4) % size) ^ crossed,
            (me + 2) % size,
            (me + 4) % size,
        ]
    ).astype(I32)
    row_lanes = (capacity // 128 + 1) * 128
    partial = call(
        functools.partial(last_kernel, capacity),
        shape((size, row_lanes), F32),
        [SMEM] + [VMEM] * 10,
        5 * product,
        6 * block_bytes,
    )(targets, over, own_best, twin_best, next_best, block, twin, back, back_twin, far, far_ahead)
    everyone = lax.all_to_all(partial, "narrow", split_axis=0, concat_axis=0, tiled=True)
    answers = call(
        functools.partial(answer_kernel, capacity),
        shape((groups, lanes), F32),
        [VMEM] * 2,
        slots * slots * 8,
        groups * lanes * 8,
    )(everyone, position)
    answers = lax.all_to_all(answers, "wide", split_axis=0, concat_axis=0, tiled=True)
    return call(
        home_kernel,
        (shape(slot.shape, F32), shape((1, 128), I32)),
        [VMEM] * 2,
        slots * slot.shape[1] * 4,
        groups * lanes * 4,
    )(slot, answers)


def shards(embeddings, labels):
    docs, width = embeddings.shape
    groups = lax.axis_size("wide")
    lanes = 128
    tall = CAP * width // lanes + 8
    shape = jax.ShapeDtypeStruct
    offset = (lax.axis_index("wide") % (lanes // CAP) * CAP).astype(I32).reshape(1)
    outgoing, slot = call(
        place_kernel,
        (shape((groups, tall, lanes), BF16), shape((1, docs), I32)),
        [SMEM, VMEM, VMEM],
        2 * groups * CAP * docs * width,
        2 * docs * width + 2 * groups * tall * lanes,
    )(offset, embeddings, labels.reshape(1, docs))
    received = lax.all_to_all(outgoing, "wide", split_axis=0, concat_axis=0, tiled=True)
    quick, over = nearest(received, slot, 336)
    result = lax.cond(
        over[0, 0] > 0,
        lambda rows, places, unused: nearest(rows, places, groups * CAP)[0],
        lambda rows, places, done: done,
        received,
        slot,
        quick,
    )
    return result.reshape(docs)


def solution(mesh):
    in_specs = (P(("wide", "narrow"), None), P(("wide", "narrow")))
    out_specs = P(("wide", "narrow"))
    return jax.shard_map(shards, mesh=mesh, in_specs=in_specs, out_specs=out_specs, check_vma=False)
```

time: 241 us -> 129 us (0.54)
  waiting for transfers between devices: 75.7 us -> 29.6 us
  matrix products: 38.5 us -> 0 us
  local copies, waits for them, and re-layouts: 17.6 us -> 1.84 us
  between operations: 13.5 us -> 0.38 us
  Pallas kernels: 0 us -> 9.85 us
  loops' own time: 9.68 us -> 0.23 us
  starting transfers between devices: 18.5 us -> 27.5 us
  other arithmetic: 8.24 us -> 0 us
    all_gather x1 -> x0, waiting for transfers between devices: 58.5 us -> none  [shards(): lax.all_gather(rows, 'narrow', axis=0, tiled=True)]
    dot_general x16 -> x0, matrix products: 38.5 us -> none  [masked_scores(): lax.dot_general(left, right, (((1,), (1,)), ((), ())), preferred_element_...]
    ppermute x0 -> x6, starting transfers between devices: none -> 23 us  [the longest x1 4.85 us: nearest(): far_ahead = lax.ppermute(ahead, 'narrow', ring(-1))]
    ppermute x0 -> x6, waiting for transfers between devices: none -> 20.9 us  [the longest x1 9.2 us: nearest(): far_ahead = lax.ppermute(ahead, 'narrow', ring(-1))]
    all_gather x1 -> x0, blocking collectives: 20.1 us -> none  [shards(): lax.all_gather(row_labels, 'narrow', axis=0, tiled=True)]
    all_to_all x0 -> x1, blocking collectives: none -> 15.3 us  [nearest(): lax.all_to_all(partial, 'narrow', split_axis=0, concat_axis=0, tiled=True)]
    all_to_all x2 -> x1, starting transfers between devices: 18.5 us -> 4.52 us  [nearest(): lax.all_to_all(answers, 'wide', split_axis=0, concat_axis=0, tiled=True)]
    dynamic_slice x32 -> x0, local copies, waits for them, and re-layouts: 10.7 us -> none  [the longest x16 9.42 us: fold_piece(): lax.scan(advance, best, jnp.arange(amount // stride, dtype=jnp.int32))]
  transfers between devices with their start and end apart: 3 -> 7, of which waited for: 3 -> 4; matrix products, arithmetic and copies ran while one was open for 1% -> 0% of each run, Pallas kernels for 0% -> 2%
where the time goes in v1:
time: 129 us
  blocking collectives  59.2 us (46%)
  waiting for transfers between devices  29.6 us (23%)
  starting transfers between devices  27.5 us (21%)
  Pallas kernels  9.85 us (8%)
  local copies, waits for them, and re-layouts  1.84 us (1%)
    all_to_all x1, blocking collectives, shards(): lax.all_to_all(outgoing, 'wide', split_axis=0, concat_axis=0, tiled=True)  43.9 us
    all_to_all x1, blocking collectives, nearest(): lax.all_to_all(partial, 'narrow', split_axis=0, concat_axis=0, tiled=True)  15.3 us
    ppermute x1, waiting for transfers between devices, nearest(): far_ahead = lax.ppermute(ahead, 'narrow', ring(-1))  9.2 us
    all_to_all x1, waiting for transfers between devices, nearest(): lax.all_to_all(answers, 'wide', split_axis=0, concat_axis=0, tiled=True)  8.62 us
    ppermute x1, waiting for transfers between devices, nearest(): back = lax.ppermute(block, 'narrow', ring(1))  7.81 us
    ppermute x1, starting transfers between devices, nearest(): far_ahead = lax.ppermute(ahead, 'narrow', ring(-1))  4.85 us
    ppermute x1, starting transfers between devices, nearest(): back_twin = lax.ppermute(back, 'narrow', twins)  4.8 us
    all_to_all x1, starting transfers between devices, nearest(): lax.all_to_all(answers, 'wide', split_axis=0, concat_axis=0, tiled=True)  4.52 us
  transfers between devices with their start and end apart: 7, of which 4 were waited for; matrix products, arithmetic and copies ran while one was open for 0% of the time, Pallas kernels for 2%

profile of v1, /device:TPU:1, one launch (start us, length us, event | category | flops | bytes accessed | tf_op | source)
XLA Modules:
  0.0 128.6 jit_solution(3235514941896861072)
XLA Ops:
  0.0 0.0 copy-start
  0.0 1.0 copy-done
  1.0 0.0 copy-start.1
  1.0 0.7 copy-done.1
  1.7 0.7 shard_map.30
  2.4 43.9 %all_to_all.45.in_ref = bf16[32,136,128]{2,1,0:T(8,128)(2,1)S(1)} all-to-all(bf16[32,136,128]{2,1,0:T(8,128)(2,1)S(1)} %get-tuple-element.35), channel_id=1, replica_groups=mesh['wide'=32,'narrow'=16] {'wide'}, dimensions={0} | all-to-all | bytes 2228224 | tf_op jit(solution)/shard_map/all_to_all | solution.py:301
  46.3 0.0 copy-start.2
  46.3 1.1 shard_map.31
  47.4 3.2 %collective-permute-start.8 = (bf16[352,1024]{1,0:T(8,128)(2,1)S(1)}, bf16[352,1024]{1,0:T(8,128)(2,1)S(1)}, u32[]{:S(2)}, u32[]{:S(2)}) collective-permute-start(bf16[352,1024]{1,0:T(8,128)(2,1)S(1)} %get-tuple-element.37.own_ref), channel_id=1, source_target_pairs={{0,2},{1,3},{2,4},{3,5},{4,6},{5,7},{6,8},{7,9},{8,10},{9,11},{10,... | collective-permute-start | bytes 2162696 | tf_op jit(solution)/shard_map/ppermute | solution.py:230
  50.6 3.8 %collective-permute-start.7 = (bf16[352,1024]{1,0:T(8,128)(2,1)S(1)}, bf16[352,1024]{1,0:T(8,128)(2,1)S(1)}, u32[]{:S(2)}, u32[]{:S(2)}) collective-permute-start(bf16[352,1024]{1,0:T(8,128)(2,1)S(1)} %get-tuple-element.37.own_ref), channel_id=1, source_target_pairs={{0,14},{1,15},{2,0},{3,1},{4,2},{5,3},{6,4},{7,5},{8,6},{9,7},{10,... | collective-permute-start | bytes 2162696 | tf_op jit(solution)/shard_map/ppermute | solution.py:231
  54.4 4.4 %collective-permute-start.6 = (bf16[352,1024]{1,0:T(8,128)(2,1)S(1)}, bf16[352,1024]{1,0:T(8,128)(2,1)S(1)}, u32[]{:S(2)}, u32[]{:S(2)}) collective-permute-start(bf16[352,1024]{1,0:T(8,128)(2,1)S(1)} %get-tuple-element.37.own_ref), channel_id=1, source_target_pairs={{0,1},{1,0},{2,3},{3,2},{4,5},{5,4},{6,7},{7,6},{8,9},{9,8},{10,11... | collective-permute-start | bytes 2162696 | tf_op jit(solution)/shard_map/ppermute | solution.py:232
  58.9 7.8 %collective-permute-done.8.back_ref = bf16[352,1024]{1,0:T(8,128)(2,1)S(1)} collective-permute-done((bf16[352,1024]{1,0:T(8,128)(2,1)S(1)}, bf16[352,1024]{1,0:T(8,128)(2,1)S(1)}, u32[]{:S(2)}, u32[]{:S(2)}) %collective-permute-start.8) | collective-permute-done | bytes 720928 | tf_op jit(solution)/shard_map/ppermute | solution.py:230
  66.7 1.9 %collective-permute-start.10 = (bf16[352,1024]{1,0:T(8,128)(2,1)S(1)}, bf16[352,1024]{1,0:T(8,128)(2,1)}, u32[]{:S(2)}, u32[]{:S(2)}) collective-permute-start(bf16[352,1024]{1,0:T(8,128)(2,1)S(1)} %collective-permute-done.8.back_ref), channel_id=1, source_target_pairs={{0,2},{1,3},{2,4},{3,5},{4,6},{5,7},{6,9},{7,8},{8,11},{9,10},{10,... | collective-permute-start | bytes 2162696 | tf_op jit(solution)/shard_map/ppermute | solution.py:233
  68.6 4.8 %collective-permute-start.9 = (bf16[352,1024]{1,0:T(8,128)(2,1)S(1)}, bf16[352,1024]{1,0:T(8,128)(2,1)}, u32[]{:S(2)}, u32[]{:S(2)}) collective-permute-start(bf16[352,1024]{1,0:T(8,128)(2,1)S(1)} %collective-permute-done.8.back_ref), channel_id=1, source_target_pairs={{0,1},{1,0},{2,3},{3,2},{4,5},{5,4},{6,7},{7,6},{8,9},{9,8},{10,11... | collective-permute-start | bytes 2162696 | tf_op jit(solution)/shard_map/ppermute | solution.py:235
  73.4 0.0 collective-permute-done.7.next_ref
  73.4 0.0 copy-done.2
  73.4 4.9 %collective-permute-start.11 = (bf16[352,1024]{1,0:T(8,128)(2,1)S(1)}, bf16[352,1024]{1,0:T(8,128)(2,1)}, u32[]{:S(2)}, u32[]{:S(2)}) collective-permute-start(bf16[352,1024]{1,0:T(8,128)(2,1)S(1)} %collective-permute-done.7.next_ref), channel_id=1, source_target_pairs={{0,14},{1,15},{2,0},{3,1},{4,2},{5,3},{6,4},{7,5},{8,6},{9,7},{10,... | collective-permute-start | bytes 2162696 | tf_op jit(solution)/shard_map/ppermute | solution.py:234
  78.3 0.1 stack.55.targets_ref
  78.4 0.0 collective-permute-done.6.twin_ref
  78.4 1.1 shard_map.32.best_ref
  79.5 1.2 shard_map.33
  80.7 3.9 %collective-permute-done.10.far_ref = bf16[352,1024]{1,0:T(8,128)(2,1)} collective-permute-done((bf16[352,1024]{1,0:T(8,128)(2,1)S(1)}, bf16[352,1024]{1,0:T(8,128)(2,1)}, u32[]{:S(2)}, u32[]{:S(2)}) %collective-permute-start.10) | collective-permute-done | bytes 720928 | tf_op jit(solution)/shard_map/ppermute | solution.py:233
  84.6 0.0 collective-permute-done.9.back_twin_ref
  84.6 9.2 %collective-permute-done.11.ahead_ref = bf16[352,1024]{1,0:T(8,128)(2,1)} collective-permute-done((bf16[352,1024]{1,0:T(8,128)(2,1)S(1)}, bf16[352,1024]{1,0:T(8,128)(2,1)}, u32[]{:S(2)}, u32[]{:S(2)}) %collective-permute-start.11) | collective-permute-done | bytes 720928 | tf_op jit(solution)/shard_map/ppermute | solution.py:234
  93.8 4.0 %shard_map.34 = f32[16,384]{1,0:T(8,128)S(1)} custom-call(s32[7]{0:T(128)S(1)} %stack.55.targets_ref, f32[1,128]{1,0:T(1,128)S(1)} %get-tuple-element.36.over_ref, f32[1,336]{1,0:T(1,128)S(1)} %get-tuple-element.38.own_best, f32[1,336]{1,0:T(1,128)S(1)} %get-tuple-element.39.twin_best, f32[1,336]{1,0:T(1,128)S(1)} %get-tuple-element.40.next_best, ...), custom_call_target="tpu_custom_call" | custom-call | flops 1300561920 | bytes 4325376 | tf_op jit(solution)/shard_map/pallas_call | solution.py:262
  97.9 15.3 %all_to_all.46 = f32[16,1,384]{2,1,0:T(1,128)S(1)} all-to-all(f32[16,1,384]{2,1,0:T(1,128)S(1)} %copy.7), channel_id=1, replica_groups=mesh['wide'=32,'narrow'=16] {'narrow'}, dimensions={0} | all-to-all | bytes 49152 | tf_op jit(solution)/shard_map/all_to_all | solution.py:269
  113.2 1.1 shard_map.35
  114.2 4.5 %all-to-all-start.4 = ((f32[32,1,128]{2,1,0:T(1,128)}), f32[32,1,128]{2,1,0:T(1,128)S(1)}, u32[]{:S(2)}, u32[]{:S(2)}) async-start(f32[32,1,128]{2,1,0:T(1,128)} %bitcast.25), calls=%async_computation.4 | async-start | bytes 32768 | tf_op jit(solution)/shard_map/all_to_all | solution.py:277
  118.8 8.6 %all-to-all-done.4 = f32[32,1,128]{2,1,0:T(1,128)S(1)} async-done(((f32[32,1,128]{2,1,0:T(1,128)}), f32[32,1,128]{2,1,0:T(1,128)S(1)}, u32[]{:S(2)}, u32[]{:S(2)}) %all-to-all-start.4) | async-done | bytes 16416 | tf_op jit(solution)/shard_map/all_to_all | solution.py:277
  127.4 0.8 shard_map.36
  128.2 0.2 conditional.1
  (2 shorter events, 0.0 us)
Async XLA Ops:
  0.0 1.0 copy-start
  1.0 0.7 copy-start.1
  46.3 27.1 %copy-start.2 = (bf16[32,136,128]{2,1,0:T(8,128)(2,1)}, bf16[32,136,128]{2,1,0:T(8,128)(2,1)S(1)}, u32[]{:S(2)}) copy-start(bf16[32,136,128]{2,1,0:T(8,128)(2,1)S(1)} %all_to_all.45.in_ref) | copy-start | bytes 3342340
  47.4 19.3 %collective-permute-start.8 = (bf16[352,1024]{1,0:T(8,128)(2,1)S(1)}, bf16[352,1024]{1,0:T(8,128)(2,1)S(1)}, u32[]{:S(2)}, u32[]{:S(2)}) collective-permute-start(bf16[352,1024]{1,0:T(8,128)(2,1)S(1)} %get-tuple-element.37.own_ref), channel_id=1, source_target_pairs={{0,2},{1,3},{2,4},{3,5},{4,6},{5,7},{6,8},{7,9},{8,10},{9,11},{10,... | collective-permute-start | bytes 2162696 | tf_op jit(solution)/shard_map/ppermute | solution.py:230
  50.6 22.8 %collective-permute-start.7 = (bf16[352,1024]{1,0:T(8,128)(2,1)S(1)}, bf16[352,1024]{1,0:T(8,128)(2,1)S(1)}, u32[]{:S(2)}, u32[]{:S(2)}) collective-permute-start(bf16[352,1024]{1,0:T(8,128)(2,1)S(1)} %get-tuple-element.37.own_ref), channel_id=1, source_target_pairs={{0,14},{1,15},{2,0},{3,1},{4,2},{5,3},{6,4},{7,5},{8,6},{9,7},{10,... | collective-permute-start | bytes 2162696 | tf_op jit(solution)/shard_map/ppermute | solution.py:231
  54.4 24.0 %collective-permute-start.6 = (bf16[352,1024]{1,0:T(8,128)(2,1)S(1)}, bf16[352,1024]{1,0:T(8,128)(2,1)S(1)}, u32[]{:S(2)}, u32[]{:S(2)}) collective-permute-start(bf16[352,1024]{1,0:T(8,128)(2,1)S(1)} %get-tuple-element.37.own_ref), channel_id=1, source_target_pairs={{0,1},{1,0},{2,3},{3,2},{4,5},{5,4},{6,7},{7,6},{8,9},{9,8},{10,11... | collective-permute-start | bytes 2162696 | tf_op jit(solution)/shard_map/ppermute | solution.py:232
  66.7 17.9 %collective-permute-start.10 = (bf16[352,1024]{1,0:T(8,128)(2,1)S(1)}, bf16[352,1024]{1,0:T(8,128)(2,1)}, u32[]{:S(2)}, u32[]{:S(2)}) collective-permute-start(bf16[352,1024]{1,0:T(8,128)(2,1)S(1)} %collective-permute-done.8.back_ref), channel_id=1, source_target_pairs={{0,2},{1,3},{2,4},{3,5},{4,6},{5,7},{6,9},{7,8},{8,11},{9,10},{10,... | collective-permute-start | bytes 2162696 | tf_op jit(solution)/shard_map/ppermute | solution.py:233
  68.6 16.0 %collective-permute-start.9 = (bf16[352,1024]{1,0:T(8,128)(2,1)S(1)}, bf16[352,1024]{1,0:T(8,128)(2,1)}, u32[]{:S(2)}, u32[]{:S(2)}) collective-permute-start(bf16[352,1024]{1,0:T(8,128)(2,1)S(1)} %collective-permute-done.8.back_ref), channel_id=1, source_target_pairs={{0,1},{1,0},{2,3},{3,2},{4,5},{5,4},{6,7},{7,6},{8,9},{9,8},{10,11... | collective-permute-start | bytes 2162696 | tf_op jit(solution)/shard_map/ppermute | solution.py:235
  73.4 20.4 %collective-permute-start.11 = (bf16[352,1024]{1,0:T(8,128)(2,1)S(1)}, bf16[352,1024]{1,0:T(8,128)(2,1)}, u32[]{:S(2)}, u32[]{:S(2)}) collective-permute-start(bf16[352,1024]{1,0:T(8,128)(2,1)S(1)} %collective-permute-done.7.next_ref), channel_id=1, source_target_pairs={{0,14},{1,15},{2,0},{3,1},{4,2},{5,3},{6,4},{7,5},{8,6},{9,7},{10,... | collective-permute-start | bytes 2162696 | tf_op jit(solution)/shard_map/ppermute | solution.py:234
  114.2 13.1 %all-to-all-start.4 = ((f32[32,1,128]{2,1,0:T(1,128)}), f32[32,1,128]{2,1,0:T(1,128)S(1)}, u32[]{:S(2)}, u32[]{:S(2)}) async-start(f32[32,1,128]{2,1,0:T(1,128)} %bitcast.25), calls=%async_computation.4 | async-start | bytes 32768 | tf_op jit(solution)/shard_map/all_to_all | solution.py:277

commit v2 on v1

v2 whole, which is shorter than its diff:
```python
import functools
import math

import jax
import jax.numpy as jnp
from jax import lax
from jax.experimental import pallas as pl
from jax.experimental.pallas import tpu as pltpu
from jax.sharding import PartitionSpec as P

CL_GROUP = 4
CAP = 16
LIFT = 4.0
LABEL_ROWS = 16
F32, BF16, I32 = jnp.float32, jnp.bfloat16, jnp.int32
NT = (((1,), (1,)), ((), ()))
NN = (((1,), (0,)), ((), ()))
TN = (((0,), (0,)), ((), ()))
VMEM = pl.BlockSpec(memory_space=pltpu.VMEM)
SMEM = pl.BlockSpec(memory_space=pltpu.SMEM)


def dot(a, b, dims):
    return lax.dot_general(a, b, dims, preferred_element_type=F32)


def iota(shape, dim):
    return lax.broadcasted_iota(I32, shape, dim)


def one_hot(condition):
    return condition.astype(F32).astype(BF16)


def call(kernel, out_shape, in_specs, flops, size):
    return pl.pallas_call(
        kernel,
        out_shape=out_shape,
        in_specs=in_specs,
        out_specs=jax.tree.map(lambda _: VMEM, out_shape),
        compiler_params=pltpu.CompilerParams(vmem_limit_bytes=24 * 1024 * 1024),
        cost_estimate=pl.CostEstimate(flops=flops, bytes_accessed=size, transcendentals=0),
    )


def place_kernel(offset_ref, rows_ref, labels_ref, out_ref, slot_ref):
    docs, width = rows_ref.shape
    groups, tall, lanes = out_ref.shape
    labels = labels_ref[...]
    owner = labels >> 2
    mine = iota((groups, docs), 0) == owner
    before = one_hot(iota((docs, docs), 0) < iota((docs, docs), 1))
    earlier = dot(one_hot(mine), before, NN)
    rank = jnp.sum(jnp.where(mine, earlier, 0.0), axis=0, keepdims=True).astype(I32)
    slot = owner * CAP + rank
    slot_ref[...] = slot
    values = rows_ref[...].astype(F32)
    mean = jnp.mean(values * values, axis=1, keepdims=True)
    unit = (values * lax.rsqrt(mean + 1e-06) / math.sqrt(width)).astype(BF16)
    pick = one_hot(iota((groups * CAP, docs), 0) == slot)
    step = 2 * lanes
    for first in range(0, width, step):
        placed = dot(pick, unit[:, first : first + step], NN).astype(BF16)
        for half in range(2):
            k = first // lanes + half
            part = placed[:, half * lanes : (half + 1) * lanes]
            out_ref[:, k * CAP : (k + 1) * CAP, :] = part.reshape(groups, CAP, lanes)
    below = tall - CAP * width // lanes
    index = iota((groups * below, docs), 0)
    cluster = index & (below - 1)
    wanted = (labels == (index >> 3) * CL_GROUP + cluster) & (cluster < CL_GROUP)
    lane = one_hot(iota((lanes, docs), 0) == rank + offset_ref[0])
    flags = dot(one_hot(wanted), lane, NT).astype(BF16)
    out_ref[:, tall - below :, :] = flags.reshape(groups, below, lanes)


def compact_kernel(capacity, in_ref, out_ref, position_ref):
    groups, tall, lanes = in_ref.shape
    width = out_ref.shape[1]
    count = width // lanes
    slots = groups * CAP
    below = tall - CAP * count
    labels = in_ref[:, tall - below :, :].astype(F32)
    per = lanes // CAP
    labels = jnp.sum(labels.reshape(groups // per, per, below, lanes), axis=1)
    labels = jnp.concatenate([labels[i] for i in range(groups // per)], axis=1)
    valid = jnp.sum(labels, axis=0, keepdims=True)
    before = one_hot(iota((slots, slots), 0) < iota((slots, slots), 1))
    rank = dot(jnp.broadcast_to(valid, (8, slots)).astype(BF16), before, NN)[:1]
    position = jnp.where(valid > 0.5, rank.astype(I32), -1)
    position_ref[...] = position
    total = jnp.sum(valid, axis=1, keepdims=True)
    over = jnp.broadcast_to(jnp.where(total > capacity + 0.5, 1.0, 0.0), (below, lanes))
    pick = one_hot(iota((capacity, slots), 0) == position)
    for k in range(count):
        part = in_ref[:, k * CAP : (k + 1) * CAP, :].reshape(slots, lanes)
        out_ref[:capacity, k * lanes : (k + 1) * lanes] = dot(pick, part, NN).astype(BF16)
    marks = dot(labels.astype(BF16), pick, NT).astype(BF16)
    marks = jnp.concatenate([marks, jnp.zeros((below, width - capacity), BF16)], axis=1)
    flag = jnp.concatenate([jnp.zeros((below, width - lanes), F32), over], axis=1).astype(BF16)
    out_ref[capacity:, :] = jnp.concatenate([marks, flag], axis=0)


def best_of(ref, others, capacity, skip_self=False):
    rows = ref[:capacity, :]
    marks = (ref[capacity:, :capacity].astype(F32) * LIFT).astype(BF16)
    best = None
    for other in others:
        if isinstance(other, tuple):
            other = jnp.concatenate([part[...] for part in other], axis=0)
        scores = dot(other[:capacity, :], rows, NT) + dot(other[capacity:, :capacity], marks, TN)
        if skip_self and other is ref:
            same = iota((capacity, capacity), 0) == iota((capacity, capacity), 1)
            scores = jnp.where(same, -9.0, scores)
        column = jnp.max(scores, axis=0, keepdims=True)
        best = column if best is None else jnp.maximum(best, column)
    return best


def near_kernel(
    capacity, own_ref, twin_ref, a_ref, a_twin_ref, b_ref, b_twin_ref, position_ref, out_ref, column_ref
):
    others = (own_ref, twin_ref, a_ref, a_twin_ref, b_ref, b_twin_ref)
    out_ref[...] = best_of(own_ref, others, capacity, skip_self=True)
    slots = position_ref.shape[1]
    diagonal = iota((slots, slots), 0) == iota((slots, slots), 1)
    column = jnp.max(jnp.where(diagonal, position_ref[...], -1), axis=1, keepdims=True)
    column_ref[...] = jnp.broadcast_to(column, column_ref.shape)


def report_kernel(capacity, rows_ref, seen_ref, *refs):
    *others, out_ref = refs
    if len(others) > 5:
        others[4:] = [tuple(others[4:])]
    lanes = 128
    width = rows_ref.shape[1]
    flags = jnp.broadcast_to(seen_ref[:, capacity : capacity + 1], (1, lanes))
    for ref in (rows_ref, *others):
        ref = ref[-1] if isinstance(ref, tuple) else ref
        seen = ref[ref.shape[0] - LABEL_ROWS :, width - lanes :].astype(F32)
        flags = jnp.maximum(flags, jnp.max(seen, axis=0, keepdims=True))
    flags = flags[:, : out_ref.shape[1] - capacity]
    out_ref[...] = jnp.concatenate([best_of(rows_ref, others, capacity), flags], axis=1)


def answer_kernel(capacity, near_ref, seen_ref, told_a, told_b, position_ref, out_ref):
    slots = position_ref.shape[0]
    groups, lanes = out_ref.shape
    told = jnp.maximum(told_a[...], told_b[...])
    over = jnp.maximum(told, seen_ref[...])[:, capacity : capacity + 1]
    best = jnp.maximum(jnp.maximum(near_ref[...], told[:, :capacity]) - LIFT, -1.0)
    hit = iota((slots, capacity), 1) == position_ref[:, :1]
    values = jnp.max(jnp.where(hit, best, -1.0), axis=1, keepdims=True)
    values = jnp.broadcast_to(values, (slots, lanes)).reshape(groups, CAP, lanes)
    same = iota((groups, CAP, lanes), 1) == iota((groups, CAP, lanes), 2)
    answers = jnp.max(jnp.where(same, values, -1.0), axis=1)
    out_ref[...] = jnp.where(iota((groups, lanes), 1) == CAP, over, answers)


def home_kernel(slot_ref, answers_ref, out_ref, over_ref):
    groups, lanes = answers_ref.shape
    docs = slot_ref.shape[1]
    answers = answers_ref[...]
    over = jnp.max(answers[:, CAP : CAP + 1], axis=0, keepdims=True)
    over_ref[...] = jnp.broadcast_to((over > 0.5).astype(I32), over_ref.shape)
    spread = jnp.broadcast_to(answers[:, None, :], (groups, CAP, lanes))
    same = iota((groups, CAP, lanes), 1) == iota((groups, CAP, lanes), 2)
    column = jnp.max(jnp.where(same, spread, -1.0), axis=2, keepdims=True)
    column = column.reshape(groups * CAP, 1)
    hit = iota((groups * CAP, docs), 0) == slot_ref[...]
    out_ref[...] = jnp.max(jnp.where(hit, column, -1.0), axis=0, keepdims=True)


def turn(step):
    size = lax.axis_size("narrow")
    return [(i, (i + 2 * (step if i % 2 == 0 else -step)) % size) for i in range(size)]


def nearest(received, slot, capacity):
    width = 1024
    groups, tall, lanes = received.shape
    slots = groups * CAP
    size = lax.axis_size("narrow")
    shape = jax.ShapeDtypeStruct
    block_bytes = 2 * (capacity + LABEL_ROWS) * width
    product = 2 * capacity * capacity * (width + 128)
    line = shape((1, capacity), F32)
    block, position = call(
        functools.partial(compact_kernel, capacity),
        (shape((capacity + LABEL_ROWS, width), BF16), shape((1, slots), I32)),
        [VMEM],
        2 * capacity * slots * width,
        received.size * 2 + block_bytes,
    )(received)

    def send(rows, pairs):
        return lax.ppermute(rows, "narrow", pairs)

    twins = [(i, i ^ 1) for i in range(size)]
    a = send(block, turn(-1))
    b = send(block, turn(1))
    twin = send(block, twins)
    a, twin = lax.optimization_barrier((a, twin))
    a2 = send(a, turn(-1))
    b_twin = send(a, twins)
    b2 = send(b, turn(1))
    a_twin = send(b, twins)
    half = (capacity + LABEL_ROWS) // 32 * 16
    b2_twin = [send(a2[:half], twins), send(a2[half:], twins)]

    near, column = call(
        functools.partial(near_kernel, capacity),
        (line, shape((slots, lanes), I32)),
        [VMEM] * 7,
        6 * product,
        6 * block_bytes,
    )(block, twin, a, a_twin, b, b_twin, position)
    told = shape((1, (capacity // 128 + 1) * 128), F32)
    def report(*refs):
        kernel = functools.partial(report_kernel, capacity)
        return call(kernel, told, [VMEM] * len(refs), 5 * product, 6 * block_bytes)(*refs)

    to_a2 = report(a2, jnp.zeros(told.shape, F32), block, twin, b, b_twin, *b2_twin)
    to_b2 = report(b2, to_a2, block, twin, a, a_twin, a2)
    told_a = send(to_a2, turn(2))
    told_b = send(to_b2, turn(-2))
    answers = call(
        functools.partial(answer_kernel, capacity),
        shape((groups, lanes), F32),
        [VMEM] * 5,
        slots * slots * 8,
        groups * lanes * 8,
    )(near, to_b2, told_a, told_b, column)
    answers = lax.all_to_all(answers, "wide", split_axis=0, concat_axis=0, tiled=True)
    return call(
        home_kernel,
        (shape(slot.shape, F32), shape((1, 128), I32)),
        [VMEM] * 2,
        slots * slot.shape[1] * 4,
        groups * lanes * 4,
    )(slot, answers)


def shards(embeddings, labels):
    docs, width = embeddings.shape
    groups = lax.axis_size("wide")
    lanes = 128
    tall = CAP * width // lanes + 8
    shape = jax.ShapeDtypeStruct
    offset = (lax.axis_index("wide") % (lanes // CAP) * CAP).astype(I32).reshape(1)
    outgoing, slot = call(
        place_kernel,
        (shape((groups, tall, lanes), BF16), shape((1, docs), I32)),
        [SMEM, VMEM, VMEM],
        2 * groups * CAP * docs * width,
        2 * docs * width + 2 * groups * tall * lanes,
    )(offset, embeddings, labels.reshape(1, docs))
    received = lax.all_to_all(outgoing, "wide", split_axis=0, concat_axis=0, tiled=True)
    quick, over = nearest(received, slot, 336)
    result = lax.cond(
        over[0, 0] > 0,
        lambda rows, places, unused: nearest(rows, places, groups * CAP)[0],
        lambda rows, places, done: done,
        received,
        slot,
        quick,
    )
    return result.reshape(docs)


def solution(mesh):
    in_specs = (P(("wide", "narrow"), None), P(("wide", "narrow")))
    out_specs = P(("wide", "narrow"))
    return jax.shard_map(shards, mesh=mesh, in_specs=in_specs, out_specs=out_specs, check_vma=False)
```

time: 129 us -> 120 us (0.930)
  the two profiles are of different devices: /device:TPU:1 before, /device:TPU:8 now
where the time goes in v2:
time: 120 us
  blocking collectives  44.7 us (37%)
  starting transfers between devices  35.1 us (29%)
  waiting for transfers between devices  26.6 us (22%)
  Pallas kernels  11.1 us (9%)
  local copies, waits for them, and re-layouts  1.77 us (1%)
    all_to_all x1, blocking collectives, shards(): lax.all_to_all(outgoing, 'wide', split_axis=0, concat_axis=0, tiled=True)  44.7 us
    ppermute x11, starting transfers between devices, send(): return lax.ppermute(rows, 'narrow', pairs)  31.3 us
    ppermute x11, waiting for transfers between devices, send(): return lax.ppermute(rows, 'narrow', pairs)  16.9 us
    all_to_all x1, waiting for transfers between devices, nearest(): lax.all_to_all(answers, 'wide', split_axis=0, concat_axis=0, tiled=True)  9.76 us
    pallas_call x2, Pallas kernels, report(): call(kernel, told, [VMEM] * len(refs), 5 * product, 6 * block_bytes)(*refs)  4.83 us
    all_to_all x1, starting transfers between devices, nearest(): lax.all_to_all(answers, 'wide', split_axis=0, concat_axis=0, tiled=True)  3.77 us
    pallas_call x1, Pallas kernels, nearest(): call(functools.partial(near_kernel, capacity), (line, shape((slots, lanes...  2.87 us
  transfers between devices with their start and end apart: 12, of which 6 were waited for; matrix products, arithmetic and copies ran while one was open for 0% of the time, Pallas kernels for 6%

profile of v2, /device:TPU:8, one launch (start us, length us, event | category | flops | bytes accessed | tf_op | source)
XLA Modules:
  0.0 119.8 jit_solution(1886098050697094438)
XLA Ops:
  0.0 1.0 copy-done
  1.0 0.7 copy-done.1
  1.7 0.7 shard_map.30
  2.4 44.7 %all_to_all.25.in_ref = bf16[32,136,128]{2,1,0:T(8,128)(2,1)S(1)} all-to-all(bf16[32,136,128]{2,1,0:T(8,128)(2,1)S(1)} %get-tuple-element.35), channel_id=1, replica_groups=mesh['wide'=32,'narrow'=16] {'wide'}, dimensions={0} | all-to-all | bytes 2228224 | tf_op jit(solution)/shard_map/all_to_all | solution.py:258
  47.1 1.1 shard_map.31
  48.1 2.4 %collective-permute-start.11 = (bf16[352,1024]{1,0:T(8,128)(2,1)S(1)}, bf16[352,1024]{1,0:T(8,128)(2,1)S(1)}, u32[]{:S(2)}, u32[]{:S(2)}) collective-permute-start(bf16[352,1024]{1,0:T(8,128)(2,1)S(1)} %get-tuple-element.36.own_ref.refs_0_), channel_id=1, source_target_pairs={{0,14},{1,3},{2,0},{3,5},{4,2},{5,7},{6,4},{7,9},{8,6},{9,11},{10,... | collective-permute-start | bytes 2162696 | tf_op jit(solution)/shard_map/ppermute | solution.py:197
  50.5 1.9 %collective-permute-start.12 = (bf16[352,1024]{1,0:T(8,128)(2,1)S(1)}, bf16[352,1024]{1,0:T(8,128)(2,1)S(1)}, u32[]{:S(2)}, u32[]{:S(2)}) collective-permute-start(bf16[352,1024]{1,0:T(8,128)(2,1)S(1)} %get-tuple-element.36.own_ref.refs_0_), channel_id=1, source_target_pairs={{0,1},{1,0},{2,3},{3,2},{4,5},{5,4},{6,7},{7,6},{8,9},{9,8},{10,11... | collective-permute-start | bytes 2162696 | tf_op jit(solution)/shard_map/ppermute | solution.py:197
  52.4 3.5 %collective-permute-start.13 = (bf16[352,1024]{1,0:T(8,128)(2,1)S(1)}, bf16[352,1024]{1,0:T(8,128)(2,1)S(1)}, u32[]{:S(2)}, u32[]{:S(2)}) collective-permute-start(bf16[352,1024]{1,0:T(8,128)(2,1)S(1)} %get-tuple-element.36.own_ref.refs_0_), channel_id=1, source_target_pairs={{0,2},{1,15},{2,4},{3,1},{4,6},{5,3},{6,8},{7,5},{8,10},{9,7},{10,... | collective-permute-start | bytes 2162696 | tf_op jit(solution)/shard_map/ppermute | solution.py:197
  55.9 9.2 %collective-permute-done.11.a_ref.refs_2_ = bf16[352,1024]{1,0:T(8,128)(2,1)S(1)} collective-permute-done((bf16[352,1024]{1,0:T(8,128)(2,1)S(1)}, bf16[352,1024]{1,0:T(8,128)(2,1)S(1)}, u32[]{:S(2)}, u32[]{:S(2)}) %collective-permute-start.11) | collective-permute-done | bytes 720928 | tf_op jit(solution)/shard_map/ppermute | solution.py:197
  65.1 0.0 collective-permute-done.12.twin_ref.refs_1_
  65.1 2.4 %collective-permute-start.17 = (bf16[352,1024]{1,0:T(8,128)(2,1)S(1)}, bf16[352,1024]{1,0:T(8,128)(2,1)S(1)}, u32[]{:S(2)}, u32[]{:S(2)}) collective-permute-start(bf16[352,1024]{1,0:T(8,128)(2,1)S(1)} %collective-permute-done.11.a_ref.refs_2_), channel_id=1, source_target_pairs={{0,14},{1,3},{2,0},{3,5},{4,2},{5,7},{6,4},{7,9},{8,6},{9,11},{10,... | collective-permute-start | bytes 2162696 | tf_op jit(solution)/shard_map/ppermute | solution.py:197
  67.6 1.9 %collective-permute-start.15 = (bf16[352,1024]{1,0:T(8,128)(2,1)S(1)}, bf16[352,1024]{1,0:T(8,128)(2,1)S(1)}, u32[]{:S(2)}, u32[]{:S(2)}) collective-permute-start(bf16[352,1024]{1,0:T(8,128)(2,1)S(1)} %collective-permute-done.11.a_ref.refs_2_), channel_id=1, source_target_pairs={{0,1},{1,0},{2,3},{3,2},{4,5},{5,4},{6,7},{7,6},{8,9},{9,8},{10,11... | collective-permute-start | bytes 2162696 | tf_op jit(solution)/shard_map/ppermute | solution.py:197
  69.5 1.2 collective-permute-done.13.b_ref.refs_2_
  70.7 1.9 %collective-permute-start.14 = (bf16[352,1024]{1,0:T(8,128)(2,1)S(1)}, bf16[352,1024]{1,0:T(8,128)(2,1)S(1)}, u32[]{:S(2)}, u32[]{:S(2)}) collective-permute-start(bf16[352,1024]{1,0:T(8,128)(2,1)S(1)} %collective-permute-done.13.b_ref.refs_2_), channel_id=1, source_target_pairs={{0,1},{1,0},{2,3},{3,2},{4,5},{5,4},{6,7},{7,6},{8,9},{9,8},{10,11... | collective-permute-start | bytes 2162696 | tf_op jit(solution)/shard_map/ppermute | solution.py:197
  72.6 2.7 %collective-permute-start.16 = (bf16[352,1024]{1,0:T(8,128)(2,1)S(1)}, bf16[352,1024]{1,0:T(8,128)(2,1)S(1)}, u32[]{:S(2)}, u32[]{:S(2)}) collective-permute-start(bf16[352,1024]{1,0:T(8,128)(2,1)S(1)} %collective-permute-done.13.b_ref.refs_2_), channel_id=1, source_target_pairs={{0,2},{1,15},{2,4},{3,1},{4,6},{5,3},{6,8},{7,5},{8,10},{9,7},{10,... | collective-permute-start | bytes 2162696 | tf_op jit(solution)/shard_map/ppermute | solution.py:197
  75.4 3.6 %collective-permute-done.17.rows_ref.refs_4_ = bf16[352,1024]{1,0:T(8,128)(2,1)S(1)} collective-permute-done((bf16[352,1024]{1,0:T(8,128)(2,1)S(1)}, bf16[352,1024]{1,0:T(8,128)(2,1)S(1)}, u32[]{:S(2)}, u32[]{:S(2)}) %collective-permute-start.17) | collective-permute-done | bytes 720928 | tf_op jit(solution)/shard_map/ppermute | solution.py:197
  79.0 1.9 %collective-permute-start.18 = (bf16[176,1024]{1,0:T(8,128)(2,1)S(1)}, bf16[176,1024]{1,0:T(8,128)(2,1)S(1)}, u32[]{:S(2)}, u32[]{:S(2)}) collective-permute-start(bf16[176,1024]{1,0:T(8,128)(2,1)S(1)} %get-tuple-element.46), channel_id=1, source_target_pairs={{0,1},{1,0},{2,3},{3,2},{4,5},{5,4},{6,7},{7,6},{8,9},{9,8},{10,11... | collective-permute-start | bytes 1081352 | tf_op jit(solution)/shard_map/ppermute | solution.py:197
  81.0 2.4 %collective-permute-start.19 = (bf16[176,1024]{1,0:T(8,128)(2,1)S(1)}, bf16[176,1024]{1,0:T(8,128)(2,1)S(1)}, u32[]{:S(2)}, u32[]{:S(2)}) collective-permute-start(bf16[176,1024]{1,0:T(8,128)(2,1)S(1)} %get-tuple-element.45), channel_id=1, source_target_pairs={{0,1},{1,0},{2,3},{3,2},{4,5},{5,4},{6,7},{7,6},{8,9},{9,8},{10,11... | collective-permute-start | bytes 1081352 | tf_op jit(solution)/shard_map/ppermute | solution.py:197
  83.4 0.0 collective-permute-done.15.b_twin_ref.refs_3_
  83.4 1.3 %collective-permute-done.19.refs_5_ = bf16[176,1024]{1,0:T(8,128)(2,1)S(1)} collective-permute-done((bf16[176,1024]{1,0:T(8,128)(2,1)S(1)}, bf16[176,1024]{1,0:T(8,128)(2,1)S(1)}, u32[]{:S(2)}, u32[]{:S(2)}) %collective-permute-start.19) | collective-permute-done | bytes 360480 | tf_op jit(solution)/shard_map/ppermute | solution.py:197
  84.7 2.4 %shard_map.33.seen_ref = f32[1,384]{1,0:T(1,128)S(1)} custom-call(bf16[352,1024]{1,0:T(8,128)(2,1)S(1)} %collective-permute-done.17.rows_ref.refs_4_, f32[1,384]{1,0:T(1,128)S(1)} %broadcast_in_dim.3.seen_ref, bf16[352,1024]{1,0:T(8,128)(2,1)S(1)} %get-tuple-element.36.own_ref.refs_0_, bf16[352,1024]{1,0:T(8,128)(2,1)S(1)} %collective-permute-done.12.twin_ref.refs_1_, ...), custom_call_target="tpu_custom_call" | custom-call | flops 1300561920 | bytes 4325376 | tf_op jit(solution)/shard_map/pallas_call | solution.py:221
  87.1 8.3 %collective-permute-start.20 = (f32[1,384]{1,0:T(1,128)S(1)}, f32[1,384]{1,0:T(1,128)S(1)}, u32[]{:S(2)}, u32[]{:S(2)}) collective-permute-start(f32[1,384]{1,0:T(1,128)S(1)} %shard_map.33.seen_ref), channel_id=1, source_target_pairs={{0,4},{1,13},{2,6},{3,15},{4,8},{5,1},{6,10},{7,3},{8,12},{9,5},{1... | collective-permute-start | bytes 4616 | tf_op jit(solution)/shard_map/ppermute | solution.py:197
  95.4 0.0 collective-permute-done.16.rows_ref
  95.4 2.4 %shard_map.34.seen_ref = f32[1,384]{1,0:T(1,128)S(1)} custom-call(bf16[352,1024]{1,0:T(8,128)(2,1)S(1)} %collective-permute-done.16.rows_ref, f32[1,384]{1,0:T(1,128)S(1)} %shard_map.33.seen_ref, bf16[352,1024]{1,0:T(8,128)(2,1)S(1)} %get-tuple-element.36.own_ref.refs_0_, bf16[352,1024]{1,0:T(8,128)(2,1)S(1)} %collective-permute-done.12.twin_ref.refs_1_, ...), custom_call_target="tpu_custom_call" | custom-call | flops 1300561920 | bytes 4325376 | tf_op jit(solution)/shard_map/pallas_call | solution.py:221
  97.8 1.9 %collective-permute-start.21 = (f32[1,384]{1,0:T(1,128)S(1)}, f32[1,384]{1,0:T(1,128)S(1)}, u32[]{:S(2)}, u32[]{:S(2)}) collective-permute-start(f32[1,384]{1,0:T(1,128)S(1)} %shard_map.34.seen_ref), channel_id=1, source_target_pairs={{0,12},{1,5},{2,14},{3,7},{4,0},{5,9},{6,2},{7,11},{8,4},{9,13},{1... | collective-permute-start | bytes 4616 | tf_op jit(solution)/shard_map/ppermute | solution.py:197
  99.8 2.9 %shard_map.32 = (f32[1,336]{1,0:T(1,128)S(1)}, s32[512,128]{1,0:T(8,128)S(1)}) custom-call(bf16[352,1024]{1,0:T(8,128)(2,1)S(1)} %get-tuple-element.36.own_ref.refs_0_, bf16[352,1024]{1,0:T(8,128)(2,1)S(1)} %collective-permute-done.12.twin_ref.refs_1_, bf16[352,1024]{1,0:T(8,128)(2,1)S(1)} %collective-permute-done.11.a_ref.refs_2_, ...), custom_call_target="tpu_custom_call" | custom-call | flops 1560674304 | bytes 4325376 | tf_op jit(solution)/shard_map/pallas_call | solution.py:211
  102.7 1.6 %collective-permute-done.21.told_b = f32[1,384]{1,0:T(1,128)S(1)} collective-permute-done((f32[1,384]{1,0:T(1,128)S(1)}, f32[1,384]{1,0:T(1,128)S(1)}, u32[]{:S(2)}, u32[]{:S(2)}) %collective-permute-start.21) | collective-permute-done | bytes 1568 | tf_op jit(solution)/shard_map/ppermute | solution.py:197
  104.2 0.9 shard_map.35
  105.1 3.8 %all-to-all-start.2 = ((f32[32,1,128]{2,1,0:T(1,128)}), f32[32,1,128]{2,1,0:T(1,128)S(1)}, u32[]{:S(2)}, u32[]{:S(2)}) async-start(f32[32,1,128]{2,1,0:T(1,128)} %bitcast.9), calls=%async_computation.2 | async-start | bytes 32768 | tf_op jit(solution)/shard_map/all_to_all | solution.py:234
  108.9 9.8 %all-to-all-done.2 = f32[32,1,128]{2,1,0:T(1,128)S(1)} async-done(((f32[32,1,128]{2,1,0:T(1,128)}), f32[32,1,128]{2,1,0:T(1,128)S(1)}, u32[]{:S(2)}, u32[]{:S(2)}) %all-to-all-start.2) | async-done | bytes 16416 | tf_op jit(solution)/shard_map/all_to_all | solution.py:234
  118.6 0.8 shard_map.36
  119.4 0.2 conditional.1
  (7 shorter events, 0.1 us)
Async XLA Ops:
  0.0 1.0 copy-start
  1.0 0.7 copy-start.1
  48.1 17.0 %collective-permute-start.11 = (bf16[352,1024]{1,0:T(8,128)(2,1)S(1)}, bf16[352,1024]{1,0:T(8,128)(2,1)S(1)}, u32[]{:S(2)}, u32[]{:S(2)}) collective-permute-start(bf16[352,1024]{1,0:T(8,128)(2,1)S(1)} %get-tuple-element.36.own_ref.refs_0_), channel_id=1, source_target_pairs={{0,14},{1,3},{2,0},{3,5},{4,2},{5,7},{6,4},{7,9},{8,6},{9,11},{10,... | collective-permute-start | bytes 2162696 | tf_op jit(solution)/shard_map/ppermute | solution.py:197
  50.5 14.7 %collective-permute-start.12 = (bf16[352,1024]{1,0:T(8,128)(2,1)S(1)}, bf16[352,1024]{1,0:T(8,128)(2,1)S(1)}, u32[]{:S(2)}, u32[]{:S(2)}) collective-permute-start(bf16[352,1024]{1,0:T(8,128)(2,1)S(1)} %get-tuple-element.36.own_ref.refs_0_), channel_id=1, source_target_pairs={{0,1},{1,0},{2,3},{3,2},{4,5},{5,4},{6,7},{7,6},{8,9},{9,8},{10,11... | collective-permute-start | bytes 2162696 | tf_op jit(solution)/shard_map/ppermute | solution.py:197
  52.4 18.3 %collective-permute-start.13 = (bf16[352,1024]{1,0:T(8,128)(2,1)S(1)}, bf16[352,1024]{1,0:T(8,128)(2,1)S(1)}, u32[]{:S(2)}, u32[]{:S(2)}) collective-permute-start(bf16[352,1024]{1,0:T(8,128)(2,1)S(1)} %get-tuple-element.36.own_ref.refs_0_), channel_id=1, source_target_pairs={{0,2},{1,15},{2,4},{3,1},{4,6},{5,3},{6,8},{7,5},{8,10},{9,7},{10,... | collective-permute-start | bytes 2162696 | tf_op jit(solution)/shard_map/ppermute | solution.py:197
  65.1 13.8 %collective-permute-start.17 = (bf16[352,1024]{1,0:T(8,128)(2,1)S(1)}, bf16[352,1024]{1,0:T(8,128)(2,1)S(1)}, u32[]{:S(2)}, u32[]{:S(2)}) collective-permute-start(bf16[352,1024]{1,0:T(8,128)(2,1)S(1)} %collective-permute-done.11.a_ref.refs_2_), channel_id=1, source_target_pairs={{0,14},{1,3},{2,0},{3,5},{4,2},{5,7},{6,4},{7,9},{8,6},{9,11},{10,... | collective-permute-start | bytes 2162696 | tf_op jit(solution)/shard_map/ppermute | solution.py:197
  67.6 15.8 %collective-permute-start.15 = (bf16[352,1024]{1,0:T(8,128)(2,1)S(1)}, bf16[352,1024]{1,0:T(8,128)(2,1)S(1)}, u32[]{:S(2)}, u32[]{:S(2)}) collective-permute-start(bf16[352,1024]{1,0:T(8,128)(2,1)S(1)} %collective-permute-done.11.a_ref.refs_2_), channel_id=1, source_target_pairs={{0,1},{1,0},{2,3},{3,2},{4,5},{5,4},{6,7},{7,6},{8,9},{9,8},{10,11... | collective-permute-start | bytes 2162696 | tf_op jit(solution)/shard_map/ppermute | solution.py:197
  70.7 24.7 %collective-permute-start.14 = (bf16[352,1024]{1,0:T(8,128)(2,1)S(1)}, bf16[352,1024]{1,0:T(8,128)(2,1)S(1)}, u32[]{:S(2)}, u32[]{:S(2)}) collective-permute-start(bf16[352,1024]{1,0:T(8,128)(2,1)S(1)} %collective-permute-done.13.b_ref.refs_2_), channel_id=1, source_target_pairs={{0,1},{1,0},{2,3},{3,2},{4,5},{5,4},{6,7},{7,6},{8,9},{9,8},{10,11... | collective-permute-start | bytes 2162696 | tf_op jit(solution)/shard_map/ppermute | solution.py:197
  72.6 22.8 %collective-permute-start.16 = (bf16[352,1024]{1,0:T(8,128)(2,1)S(1)}, bf16[352,1024]{1,0:T(8,128)(2,1)S(1)}, u32[]{:S(2)}, u32[]{:S(2)}) collective-permute-start(bf16[352,1024]{1,0:T(8,128)(2,1)S(1)} %collective-permute-done.13.b_ref.refs_2_), channel_id=1, source_target_pairs={{0,2},{1,15},{2,4},{3,1},{4,6},{5,3},{6,8},{7,5},{8,10},{9,7},{10,... | collective-permute-start | bytes 2162696 | tf_op jit(solution)/shard_map/ppermute | solution.py:197
  79.0 4.4 %collective-permute-start.18 = (bf16[176,1024]{1,0:T(8,128)(2,1)S(1)}, bf16[176,1024]{1,0:T(8,128)(2,1)S(1)}, u32[]{:S(2)}, u32[]{:S(2)}) collective-permute-start(bf16[176,1024]{1,0:T(8,128)(2,1)S(1)} %get-tuple-element.46), channel_id=1, source_target_pairs={{0,1},{1,0},{2,3},{3,2},{4,5},{5,4},{6,7},{7,6},{8,9},{9,8},{10,11... | collective-permute-start | bytes 1081352 | tf_op jit(solution)/shard_map/ppermute | solution.py:197
  81.0 3.7 %collective-permute-start.19 = (bf16[176,1024]{1,0:T(8,128)(2,1)S(1)}, bf16[176,1024]{1,0:T(8,128)(2,1)S(1)}, u32[]{:S(2)}, u32[]{:S(2)}) collective-permute-start(bf16[176,1024]{1,0:T(8,128)(2,1)S(1)} %get-tuple-element.45), channel_id=1, source_target_pairs={{0,1},{1,0},{2,3},{3,2},{4,5},{5,4},{6,7},{7,6},{8,9},{9,8},{10,11... | collective-permute-start | bytes 1081352 | tf_op jit(solution)/shard_map/ppermute | solution.py:197
  87.1 17.2 %collective-permute-start.20 = (f32[1,384]{1,0:T(1,128)S(1)}, f32[1,384]{1,0:T(1,128)S(1)}, u32[]{:S(2)}, u32[]{:S(2)}) collective-permute-start(f32[1,384]{1,0:T(1,128)S(1)} %shard_map.33.seen_ref), channel_id=1, source_target_pairs={{0,4},{1,13},{2,6},{3,15},{4,8},{5,1},{6,10},{7,3},{8,12},{9,5},{1... | collective-permute-start | bytes 4616 | tf_op jit(solution)/shard_map/ppermute | solution.py:197
  97.8 6.4 %collective-permute-start.21 = (f32[1,384]{1,0:T(1,128)S(1)}, f32[1,384]{1,0:T(1,128)S(1)}, u32[]{:S(2)}, u32[]{:S(2)}) collective-permute-start(f32[1,384]{1,0:T(1,128)S(1)} %shard_map.34.seen_ref), channel_id=1, source_target_pairs={{0,12},{1,5},{2,14},{3,7},{4,0},{5,9},{6,2},{7,11},{8,4},{9,13},{1... | collective-permute-start | bytes 4616 | tf_op jit(solution)/shard_map/ppermute | solution.py:197
  105.1 13.5 %all-to-all-start.2 = ((f32[32,1,128]{2,1,0:T(1,128)}), f32[32,1,128]{2,1,0:T(1,128)S(1)}, u32[]{:S(2)}, u32[]{:S(2)}) async-start(f32[32,1,128]{2,1,0:T(1,128)} %bitcast.9), calls=%async_computation.2 | async-start | bytes 32768 | tf_op jit(solution)/shard_map/all_to_all | solution.py:234

commit v3 on v2

--- a/solution.py
+++ b/solution.py
@@ -117,30 +117,36 @@
     return best
 
 
-def near_kernel(
-    capacity, own_ref, twin_ref, a_ref, a_twin_ref, b_ref, b_twin_ref, position_ref, out_ref, column_ref
+def middle_kernel(
+    capacity, own_ref, twin_ref, a_ref, b_ref, b_twin_ref, a2_ref, position_ref,
+    near_ref, a2_best, column_ref,
 ):
-    others = (own_ref, twin_ref, a_ref, a_twin_ref, b_ref, b_twin_ref)
-    out_ref[...] = best_of(own_ref, others, capacity, skip_self=True)
+    others = (own_ref, twin_ref, a_ref, b_ref, b_twin_ref)
+    near_ref[...] = best_of(own_ref, others, capacity, skip_self=True)
+    a2_best[...] = best_of(a2_ref, (own_ref, twin_ref, b_ref, b_twin_ref), capacity)
     slots = position_ref.shape[1]
     diagonal = iota((slots, slots), 0) == iota((slots, slots), 1)
     column = jnp.max(jnp.where(diagonal, position_ref[...], -1), axis=1, keepdims=True)
     column_ref[...] = jnp.broadcast_to(column, column_ref.shape)
 
 
-def report_kernel(capacity, rows_ref, seen_ref, *refs):
-    *others, out_ref = refs
-    if len(others) > 5:
-        others[4:] = [tuple(others[4:])]
+def last_kernel(
+    capacity, near_best, a2_best, b2_ref, own_ref, twin_ref, a_ref, a_twin_ref, b_ref, b_twin_ref, a2_ref, *refs
+):
+    *b2_twin, to_a2, to_b2, near_ref = refs
+    near_ref[...] = jnp.maximum(near_best[...], best_of(own_ref, (a_twin_ref,), capacity))
     lanes = 128
-    width = rows_ref.shape[1]
-    flags = jnp.broadcast_to(seen_ref[:, capacity : capacity + 1], (1, lanes))
-    for ref in (rows_ref, *others):
-        ref = ref[-1] if isinstance(ref, tuple) else ref
+    width = own_ref.shape[1]
+    flags = None
+    blocks = (own_ref, twin_ref, a_ref, a_twin_ref, b_ref, b_twin_ref, a2_ref, b2_ref, b2_twin[-1])
+    for ref in blocks:
         seen = ref[ref.shape[0] - LABEL_ROWS :, width - lanes :].astype(F32)
-        flags = jnp.maximum(flags, jnp.max(seen, axis=0, keepdims=True))
-    flags = flags[:, : out_ref.shape[1] - capacity]
-    out_ref[...] = jnp.concatenate([best_of(rows_ref, others, capacity), flags], axis=1)
+        flags = seen if flags is None else jnp.maximum(flags, seen)
+    flags = jnp.max(flags, axis=0, keepdims=True)[:, : to_a2.shape[1] - capacity]
+    others = (own_ref, twin_ref, a_ref, a_twin_ref, a2_ref)
+    to_b2[...] = jnp.concatenate([best_of(b2_ref, others, capacity), flags], axis=1)
+    best = jnp.maximum(a2_best[...], best_of(a2_ref, (tuple(b2_twin),), capacity))
+    to_a2[...] = jnp.concatenate([best, flags], axis=1)
 
 
 def answer_kernel(capacity, near_ref, seen_ref, told_a, told_b, position_ref, out_ref):
@@ -200,28 +206,28 @@
     a = send(block, turn(-1))
     b = send(block, turn(1))
     twin = send(block, twins)
-    a, twin = lax.optimization_barrier((a, twin))
     a2 = send(a, turn(-1))
-    b_twin = send(a, twins)
     b2 = send(b, turn(1))
+    late_a, twin = lax.optimization_barrier((a, twin))
+    b_twin = send(late_a, twins)
     a_twin = send(b, twins)
-    half = (capacity + LABEL_ROWS) // 32 * 16
-    b2_twin = [send(a2[:half], twins), send(a2[half:], twins)]
-
-    near, column = call(
-        functools.partial(near_kernel, capacity),
-        (line, shape((slots, lanes), I32)),
+    b2_twin = [send(a2, twins)]
+    told = shape((1, (capacity // 128 + 1) * 128), F32)
+    near, a2_best, column = call(
+        functools.partial(middle_kernel, capacity),
+        (line, line, shape((slots, lanes), I32)),
         [VMEM] * 7,
-        6 * product,
-        6 * block_bytes,
-    )(block, twin, a, a_twin, b, b_twin, position)
-    told = shape((1, (capacity // 128 + 1) * 128), F32)
-    def report(*refs):
-        kernel = functools.partial(report_kernel, capacity)
-        return call(kernel, told, [VMEM] * len(refs), 5 * product, 6 * block_bytes)(*refs)
-
-    to_a2 = report(a2, jnp.zeros(told.shape, F32), block, twin, b, b_twin, *b2_twin)
-    to_b2 = report(b2, to_a2, block, twin, a, a_twin, a2)
+        9 * product,
+        7 * block_bytes,
+    )(block, twin, a, b, b_twin, a2, position)
+    blocks = (b2, block, twin, a, a_twin, b, b_twin, a2, *b2_twin)
+    to_a2, to_b2, near = call(
+        functools.partial(last_kernel, capacity),
+        (told, told, line),
+        [VMEM] * (2 + len(blocks)),
+        7 * product,
+        8 * block_bytes,
+    )(near, a2_best, *blocks)
     told_a = send(to_a2, turn(2))
     told_b = send(to_b2, turn(-2))
     answers = call(
@@ -256,7 +262,7 @@
         2 * docs * width + 2 * groups * tall * lanes,
     )(offset, embeddings, labels.reshape(1, docs))
     received = lax.all_to_all(outgoing, "wide", split_axis=0, concat_axis=0, tiled=True)
-    quick, over = nearest(received, slot, 336)
+    quick, over = nearest(received, slot, 320)
     result = lax.cond(
         over[0, 0] > 0,
         lambda rows, places, unused: nearest(rows, places, groups * CAP)[0],

time: 120 us -> 119 us (level)
  the two profiles are of different devices: /device:TPU:8 before, /device:TPU:16 now
where the time goes in v3:
time: 119 us; the launch traced here: 118 us
  blocking collectives  44.7 us (38%)
  starting transfers between devices  33.2 us (28%)
  waiting for transfers between devices  28 us (24%)
  Pallas kernels  10.3 us (9%)
  local copies, waits for them, and re-layouts  1.72 us (1%)
    all_to_all x1, blocking collectives, shards(): lax.all_to_all(outgoing, 'wide', split_axis=0, concat_axis=0, tiled=True)  44.7 us
    ppermute x10, starting transfers between devices, send(): return lax.ppermute(rows, 'narrow', pairs)  29.4 us
    ppermute x10, waiting for transfers between devices, send(): return lax.ppermute(rows, 'narrow', pairs)  18.2 us
    all_to_all x1, waiting for transfers between devices, nearest(): lax.all_to_all(answers, 'wide', split_axis=0, concat_axis=0, tiled=True)  9.79 us
    pallas_call x1, Pallas kernels, nearest(): call(functools.partial(middle_kernel, capacity), (line, line, shape((slot...  3.88 us
    all_to_all x1, starting transfers between devices, nearest(): lax.all_to_all(answers, 'wide', split_axis=0, concat_axis=0, tiled=True)  3.8 us
    pallas_call x1, Pallas kernels, nearest(): call(functools.partial(last_kernel, capacity), (told, told, line), [VMEM]...  3.06 us
  transfers between devices with their start and end apart: 11, of which 4 were waited for; matrix products, arithmetic and copies ran while one was open for 0% of the time, Pallas kernels for 3%

profile of v3, /device:TPU:16, one launch (start us, length us, event | category | flops | bytes accessed | tf_op | source)
XLA Modules:
  0.0 118.4 jit_solution(6315113159672918540)
XLA Ops:
  0.0 1.0 copy-done
  1.0 0.7 copy-done.1
  1.7 0.7 shard_map.30
  2.4 44.7 %all_to_all.25.in_ref = bf16[32,136,128]{2,1,0:T(8,128)(2,1)S(1)} all-to-all(bf16[32,136,128]{2,1,0:T(8,128)(2,1)S(1)} %get-tuple-element.43), channel_id=1, replica_groups=mesh['wide'=32,'narrow'=16] {'wide'}, dimensions={0} | all-to-all | bytes 2228224 | tf_op jit(solution)/shard_map/all_to_all | solution.py:264
  47.1 1.0 shard_map.31
  48.1 2.4 %collective-permute-start.10 = (bf16[336,1024]{1,0:T(8,128)(2,1)S(1)}, bf16[336,1024]{1,0:T(8,128)(2,1)S(1)}, u32[]{:S(2)}, u32[]{:S(2)}) collective-permute-start(bf16[336,1024]{1,0:T(8,128)(2,1)S(1)} %get-tuple-element.44.own_ref), channel_id=1, source_target_pairs={{0,14},{1,3},{2,0},{3,5},{4,2},{5,7},{6,4},{7,9},{8,6},{9,11},{10,... | collective-permute-start | bytes 2064392 | tf_op jit(solution)/shard_map/ppermute | solution.py:203
  50.5 1.9 %collective-permute-start.11 = (bf16[336,1024]{1,0:T(8,128)(2,1)S(1)}, bf16[336,1024]{1,0:T(8,128)(2,1)S(1)}, u32[]{:S(2)}, u32[]{:S(2)}) collective-permute-start(bf16[336,1024]{1,0:T(8,128)(2,1)S(1)} %get-tuple-element.44.own_ref), channel_id=1, source_target_pairs={{0,1},{1,0},{2,3},{3,2},{4,5},{5,4},{6,7},{7,6},{8,9},{9,8},{10,11... | collective-permute-start | bytes 2064392 | tf_op jit(solution)/shard_map/ppermute | solution.py:203
  52.4 3.8 %collective-permute-start.12 = (bf16[336,1024]{1,0:T(8,128)(2,1)S(1)}, bf16[336,1024]{1,0:T(8,128)(2,1)S(1)}, u32[]{:S(2)}, u32[]{:S(2)}) collective-permute-start(bf16[336,1024]{1,0:T(8,128)(2,1)S(1)} %get-tuple-element.44.own_ref), channel_id=1, source_target_pairs={{0,2},{1,15},{2,4},{3,1},{4,6},{5,3},{6,8},{7,5},{8,10},{9,7},{10,... | collective-permute-start | bytes 2064392 | tf_op jit(solution)/shard_map/ppermute | solution.py:203
  56.2 8.2 %collective-permute-done.10.a_ref = bf16[336,1024]{1,0:T(8,128)(2,1)S(1)} collective-permute-done((bf16[336,1024]{1,0:T(8,128)(2,1)S(1)}, bf16[336,1024]{1,0:T(8,128)(2,1)S(1)}, u32[]{:S(2)}, u32[]{:S(2)}) %collective-permute-start.10) | collective-permute-done | bytes 688160 | tf_op jit(solution)/shard_map/ppermute | solution.py:203
  64.4 2.3 %collective-permute-start.14 = (bf16[336,1024]{1,0:T(8,128)(2,1)S(1)}, bf16[336,1024]{1,0:T(8,128)(2,1)S(1)}, u32[]{:S(2)}, u32[]{:S(2)}) collective-permute-start(bf16[336,1024]{1,0:T(8,128)(2,1)S(1)} %collective-permute-done.10.a_ref), channel_id=1, source_target_pairs={{0,14},{1,3},{2,0},{3,5},{4,2},{5,7},{6,4},{7,9},{8,6},{9,11},{10,... | collective-permute-start | bytes 2064392 | tf_op jit(solution)/shard_map/ppermute | solution.py:203
  66.8 0.0 collective-permute-done.11.twin_ref
  66.8 1.9 %collective-permute-start.13 = (bf16[336,1024]{1,0:T(8,128)(2,1)S(1)}, bf16[336,1024]{1,0:T(8,128)(2,1)S(1)}, u32[]{:S(2)}, u32[]{:S(2)}) collective-permute-start(bf16[336,1024]{1,0:T(8,128)(2,1)S(1)} %collective-permute-done.10.a_ref), channel_id=1, source_target_pairs={{0,1},{1,0},{2,3},{3,2},{4,5},{5,4},{6,7},{7,6},{8,9},{9,8},{10,11... | collective-permute-start | bytes 2064392 | tf_op jit(solution)/shard_map/ppermute | solution.py:203
  68.7 0.0 collective-permute-done.12.b_ref
  68.7 2.4 %collective-permute-start.16 = (bf16[336,1024]{1,0:T(8,128)(2,1)S(1)}, bf16[336,1024]{1,0:T(8,128)(2,1)S(1)}, u32[]{:S(2)}, u32[]{:S(2)}) collective-permute-start(bf16[336,1024]{1,0:T(8,128)(2,1)S(1)} %collective-permute-done.12.b_ref), channel_id=1, source_target_pairs={{0,1},{1,0},{2,3},{3,2},{4,5},{5,4},{6,7},{7,6},{8,9},{9,8},{10,11... | collective-permute-start | bytes 2064392 | tf_op jit(solution)/shard_map/ppermute | solution.py:203
  71.1 4.3 %collective-permute-start.15 = (bf16[336,1024]{1,0:T(8,128)(2,1)S(1)}, bf16[336,1024]{1,0:T(8,128)(2,1)S(1)}, u32[]{:S(2)}, u32[]{:S(2)}) collective-permute-start(bf16[336,1024]{1,0:T(8,128)(2,1)S(1)} %collective-permute-done.12.b_ref), channel_id=1, source_target_pairs={{0,2},{1,15},{2,4},{3,1},{4,6},{5,3},{6,8},{7,5},{8,10},{9,7},{10,... | collective-permute-start | bytes 2064392 | tf_op jit(solution)/shard_map/ppermute | solution.py:203
  75.4 4.3 %collective-permute-done.14.a2_ref = bf16[336,1024]{1,0:T(8,128)(2,1)S(1)} collective-permute-done((bf16[336,1024]{1,0:T(8,128)(2,1)S(1)}, bf16[336,1024]{1,0:T(8,128)(2,1)S(1)}, u32[]{:S(2)}, u32[]{:S(2)}) %collective-permute-start.14) | collective-permute-done | bytes 688160 | tf_op jit(solution)/shard_map/ppermute | solution.py:203
  79.7 1.9 %collective-permute-start.17 = (bf16[336,1024]{1,0:T(8,128)(2,1)S(1)}, bf16[336,1024]{1,0:T(8,128)(2,1)S(1)}, u32[]{:S(2)}, u32[]{:S(2)}) collective-permute-start(bf16[336,1024]{1,0:T(8,128)(2,1)S(1)} %collective-permute-done.14.a2_ref), channel_id=1, source_target_pairs={{0,1},{1,0},{2,3},{3,2},{4,5},{5,4},{6,7},{7,6},{8,9},{9,8},{10,11... | collective-permute-start | bytes 2064392 | tf_op jit(solution)/shard_map/ppermute | solution.py:203
  81.6 0.0 collective-permute-done.13.b_twin_ref
  81.6 3.9 %shard_map.32 = (f32[1,320]{1,0:T(1,128)S(1)}, f32[1,320]{1,0:T(1,128)S(1)}, s32[512,128]{1,0:T(8,128)S(1)}) custom-call(bf16[336,1024]{1,0:T(8,128)(2,1)S(1)} %get-tuple-element.44.own_ref, bf16[336,1024]{1,0:T(8,128)(2,1)S(1)} %collective-permute-done.11.twin_ref, bf16[336,1024]{1,0:T(8,128)(2,1)S(1)} %collective-permute-done.10.a_ref, ...), custom_call_target="tpu_custom_call" | custom-call | flops 2123366400 | bytes 4816896 | tf_op jit(solution)/shard_map/pallas_call | solution.py:216
  85.5 0.0 collective-permute-done.16.a_twin_ref
  85.5 0.0 collective-permute-done.15.b2_ref
  85.5 0.0 collective-permute-done.17.refs_0_
  85.5 3.1 %shard_map.33 = (f32[1,384]{1,0:T(1,128)S(1)}, f32[1,384]{1,0:T(1,128)S(1)}, f32[1,320]{1,0:T(1,128)S(1)}) custom-call(f32[1,320]{1,0:T(1,128)S(1)} %get-tuple-element.48.near_best, f32[1,320]{1,0:T(1,128)S(1)} %get-tuple-element.49.a2_best, bf16[336,1024]{1,0:T(8,128)(2,1)S(1)} %collective-permute-done.15.b2_ref, ...), custom_call_target="tpu_custom_call" | custom-call | flops 1651507200 | bytes 5505024 | tf_op jit(solution)/shard_map/pallas_call | solution.py:224
  88.6 6.6 %collective-permute-start.18 = (f32[1,384]{1,0:T(1,128)S(1)}, f32[1,384]{1,0:T(1,128)S(1)}, u32[]{:S(2)}, u32[]{:S(2)}) collective-permute-start(f32[1,384]{1,0:T(1,128)S(1)} %get-tuple-element.52), channel_id=1, source_target_pairs={{0,4},{1,13},{2,6},{3,15},{4,8},{5,1},{6,10},{7,3},{8,12},{9,5},{1... | collective-permute-start | bytes 4616 | tf_op jit(solution)/shard_map/ppermute | solution.py:203
  95.2 1.9 %collective-permute-start.19 = (f32[1,384]{1,0:T(1,128)S(1)}, f32[1,384]{1,0:T(1,128)S(1)}, u32[]{:S(2)}, u32[]{:S(2)}) collective-permute-start(f32[1,384]{1,0:T(1,128)S(1)} %get-tuple-element.51.seen_ref), channel_id=1, source_target_pairs={{0,12},{1,5},{2,14},{3,7},{4,0},{5,9},{6,2},{7,11},{8,4},{9,13},{1... | collective-permute-start | bytes 4616 | tf_op jit(solution)/shard_map/ppermute | solution.py:203
  97.1 0.0 collective-permute-done.18.told_a
  97.1 5.6 %collective-permute-done.19.told_b = f32[1,384]{1,0:T(1,128)S(1)} collective-permute-done((f32[1,384]{1,0:T(1,128)S(1)}, f32[1,384]{1,0:T(1,128)S(1)}, u32[]{:S(2)}, u32[]{:S(2)}) %collective-permute-start.19) | collective-permute-done | bytes 1568 | tf_op jit(solution)/shard_map/ppermute | solution.py:203
  102.7 0.9 shard_map.34
  103.6 3.8 %all-to-all-start.2 = ((f32[32,1,128]{2,1,0:T(1,128)}), f32[32,1,128]{2,1,0:T(1,128)S(1)}, u32[]{:S(2)}, u32[]{:S(2)}) async-start(f32[32,1,128]{2,1,0:T(1,128)} %bitcast.9), calls=%async_computation.2 | async-start | bytes 32768 | tf_op jit(solution)/shard_map/all_to_all | solution.py:240
  107.4 9.8 %all-to-all-done.2 = f32[32,1,128]{2,1,0:T(1,128)S(1)} async-done(((f32[32,1,128]{2,1,0:T(1,128)}), f32[32,1,128]{2,1,0:T(1,128)S(1)}, u32[]{:S(2)}, u32[]{:S(2)}) %all-to-all-start.2) | async-done | bytes 16416 | tf_op jit(solution)/shard_map/all_to_all | solution.py:240
  117.2 0.8 shard_map.35
  118.0 0.2 conditional.1
  (2 shorter events, 0.0 us)
Async XLA Ops:
  0.0 1.0 copy-start
  1.0 0.7 copy-start.1
  48.1 16.3 %collective-permute-start.10 = (bf16[336,1024]{1,0:T(8,128)(2,1)S(1)}, bf16[336,1024]{1,0:T(8,128)(2,1)S(1)}, u32[]{:S(2)}, u32[]{:S(2)}) collective-permute-start(bf16[336,1024]{1,0:T(8,128)(2,1)S(1)} %get-tuple-element.44.own_ref), channel_id=1, source_target_pairs={{0,14},{1,3},{2,0},{3,5},{4,2},{5,7},{6,4},{7,9},{8,6},{9,11},{10,... | collective-permute-start | bytes 2064392 | tf_op jit(solution)/shard_map/ppermute | solution.py:203
  50.5 16.3 %collective-permute-start.11 = (bf16[336,1024]{1,0:T(8,128)(2,1)S(1)}, bf16[336,1024]{1,0:T(8,128)(2,1)S(1)}, u32[]{:S(2)}, u32[]{:S(2)}) collective-permute-start(bf16[336,1024]{1,0:T(8,128)(2,1)S(1)} %get-tuple-element.44.own_ref), channel_id=1, source_target_pairs={{0,1},{1,0},{2,3},{3,2},{4,5},{5,4},{6,7},{7,6},{8,9},{9,8},{10,11... | collective-permute-start | bytes 2064392 | tf_op jit(solution)/shard_map/ppermute | solution.py:203
  52.4 16.3 %collective-permute-start.12 = (bf16[336,1024]{1,0:T(8,128)(2,1)S(1)}, bf16[336,1024]{1,0:T(8,128)(2,1)S(1)}, u32[]{:S(2)}, u32[]{:S(2)}) collective-permute-start(bf16[336,1024]{1,0:T(8,128)(2,1)S(1)} %get-tuple-element.44.own_ref), channel_id=1, source_target_pairs={{0,2},{1,15},{2,4},{3,1},{4,6},{5,3},{6,8},{7,5},{8,10},{9,7},{10,... | collective-permute-start | bytes 2064392 | tf_op jit(solution)/shard_map/ppermute | solution.py:203
  64.4 15.3 %collective-permute-start.14 = (bf16[336,1024]{1,0:T(8,128)(2,1)S(1)}, bf16[336,1024]{1,0:T(8,128)(2,1)S(1)}, u32[]{:S(2)}, u32[]{:S(2)}) collective-permute-start(bf16[336,1024]{1,0:T(8,128)(2,1)S(1)} %collective-permute-done.10.a_ref), channel_id=1, source_target_pairs={{0,14},{1,3},{2,0},{3,5},{4,2},{5,7},{6,4},{7,9},{8,6},{9,11},{10,... | collective-permute-start | bytes 2064392 | tf_op jit(solution)/shard_map/ppermute | solution.py:203
  66.8 14.8 %collective-permute-start.13 = (bf16[336,1024]{1,0:T(8,128)(2,1)S(1)}, bf16[336,1024]{1,0:T(8,128)(2,1)S(1)}, u32[]{:S(2)}, u32[]{:S(2)}) collective-permute-start(bf16[336,1024]{1,0:T(8,128)(2,1)S(1)} %collective-permute-done.10.a_ref), channel_id=1, source_target_pairs={{0,1},{1,0},{2,3},{3,2},{4,5},{5,4},{6,7},{7,6},{8,9},{9,8},{10,11... | collective-permute-start | bytes 2064392 | tf_op jit(solution)/shard_map/ppermute | solution.py:203
  68.7 16.8 %collective-permute-start.16 = (bf16[336,1024]{1,0:T(8,128)(2,1)S(1)}, bf16[336,1024]{1,0:T(8,128)(2,1)S(1)}, u32[]{:S(2)}, u32[]{:S(2)}) collective-permute-start(bf16[336,1024]{1,0:T(8,128)(2,1)S(1)} %collective-permute-done.12.b_ref), channel_id=1, source_target_pairs={{0,1},{1,0},{2,3},{3,2},{4,5},{5,4},{6,7},{7,6},{8,9},{9,8},{10,11... | collective-permute-start | bytes 2064392 | tf_op jit(solution)/shard_map/ppermute | solution.py:203
  71.1 14.4 %collective-permute-start.15 = (bf16[336,1024]{1,0:T(8,128)(2,1)S(1)}, bf16[336,1024]{1,0:T(8,128)(2,1)S(1)}, u32[]{:S(2)}, u32[]{:S(2)}) collective-permute-start(bf16[336,1024]{1,0:T(8,128)(2,1)S(1)} %collective-permute-done.12.b_ref), channel_id=1, source_target_pairs={{0,2},{1,15},{2,4},{3,1},{4,6},{5,3},{6,8},{7,5},{8,10},{9,7},{10,... | collective-permute-start | bytes 2064392 | tf_op jit(solution)/shard_map/ppermute | solution.py:203
  79.7 5.8 %collective-permute-start.17 = (bf16[336,1024]{1,0:T(8,128)(2,1)S(1)}, bf16[336,1024]{1,0:T(8,128)(2,1)S(1)}, u32[]{:S(2)}, u32[]{:S(2)}) collective-permute-start(bf16[336,1024]{1,0:T(8,128)(2,1)S(1)} %collective-permute-done.14.a2_ref), channel_id=1, source_target_pairs={{0,1},{1,0},{2,3},{3,2},{4,5},{5,4},{6,7},{7,6},{8,9},{9,8},{10,11... | collective-permute-start | bytes 2064392 | tf_op jit(solution)/shard_map/ppermute | solution.py:203
  88.6 8.5 %collective-permute-start.18 = (f32[1,384]{1,0:T(1,128)S(1)}, f32[1,384]{1,0:T(1,128)S(1)}, u32[]{:S(2)}, u32[]{:S(2)}) collective-permute-start(f32[1,384]{1,0:T(1,128)S(1)} %get-tuple-element.52), channel_id=1, source_target_pairs={{0,4},{1,13},{2,6},{3,15},{4,8},{5,1},{6,10},{7,3},{8,12},{9,5},{1... | collective-permute-start | bytes 4616 | tf_op jit(solution)/shard_map/ppermute | solution.py:203
  95.2 7.6 %collective-permute-start.19 = (f32[1,384]{1,0:T(1,128)S(1)}, f32[1,384]{1,0:T(1,128)S(1)}, u32[]{:S(2)}, u32[]{:S(2)}) collective-permute-start(f32[1,384]{1,0:T(1,128)S(1)} %get-tuple-element.51.seen_ref), channel_id=1, source_target_pairs={{0,12},{1,5},{2,14},{3,7},{4,0},{5,9},{6,2},{7,11},{8,4},{9,13},{1... | collective-permute-start | bytes 4616 | tf_op jit(solution)/shard_map/ppermute | solution.py:203
  103.6 13.6 %all-to-all-start.2 = ((f32[32,1,128]{2,1,0:T(1,128)}), f32[32,1,128]{2,1,0:T(1,128)S(1)}, u32[]{:S(2)}, u32[]{:S(2)}) async-start(f32[32,1,128]{2,1,0:T(1,128)} %bitcast.9), calls=%async_computation.2 | async-start | bytes 32768 | tf_op jit(solution)/shard_map/all_to_all | solution.py:240

commit v4 on v2

--- a/solution.py
+++ b/solution.py
@@ -128,19 +128,31 @@
     column_ref[...] = jnp.broadcast_to(column, column_ref.shape)
 
 
-def report_kernel(capacity, rows_ref, seen_ref, *refs):
-    *others, out_ref = refs
-    if len(others) > 5:
-        others[4:] = [tuple(others[4:])]
-    lanes = 128
-    width = rows_ref.shape[1]
-    flags = jnp.broadcast_to(seen_ref[:, capacity : capacity + 1], (1, lanes))
-    for ref in (rows_ref, *others):
-        ref = ref[-1] if isinstance(ref, tuple) else ref
-        seen = ref[ref.shape[0] - LABEL_ROWS :, width - lanes :].astype(F32)
-        flags = jnp.maximum(flags, jnp.max(seen, axis=0, keepdims=True))
-    flags = flags[:, : out_ref.shape[1] - capacity]
-    out_ref[...] = jnp.concatenate([best_of(rows_ref, others, capacity), flags], axis=1)
+def middle_kernel(capacity, a2_ref, own_ref, twin_ref, b_ref, b_twin_ref, out_ref):
+    out_ref[...] = best_of(a2_ref, (own_ref, twin_ref, b_ref, b_twin_ref), capacity)
+
+
+def told_row(best, seen, refs, wide):
+    flags = seen
+    for ref in refs:
+        flag = ref[ref.shape[0] - LABEL_ROWS :, ref.shape[1] - 128 :].astype(F32)
+        flags = jnp.maximum(flags, jnp.max(flag, axis=0, keepdims=True))
+    return jnp.concatenate([best, flags[:, : wide - best.shape[1]]], axis=1)
+
+
+def a2_kernel(
+    capacity, a2_best, a2_ref, own_ref, twin_ref, b_ref, b_twin_ref, twin_0, twin_1, out_ref
+):
+    best = jnp.maximum(a2_best[...], best_of(a2_ref, ((twin_0, twin_1),), capacity))
+    blocks = (a2_ref, own_ref, twin_ref, b_ref, b_twin_ref, twin_1)
+    out_ref[...] = told_row(best, jnp.zeros((1, 128), F32), blocks, out_ref.shape[1])
+
+
+def b2_kernel(capacity, seen_ref, b2_ref, own_ref, twin_ref, a_ref, a_twin_ref, a2_ref, out_ref):
+    seen = jnp.broadcast_to(seen_ref[...][:, capacity : capacity + 1], (1, 128))
+    blocks = (own_ref, twin_ref, a_ref, a_twin_ref, a2_ref)
+    best = best_of(b2_ref, blocks, capacity)
+    out_ref[...] = told_row(best, seen, (b2_ref, *blocks), out_ref.shape[1])
 
 
 def answer_kernel(capacity, near_ref, seen_ref, told_a, told_b, position_ref, out_ref):
@@ -200,14 +212,23 @@
     a = send(block, turn(-1))
     b = send(block, turn(1))
     twin = send(block, twins)
-    a, twin = lax.optimization_barrier((a, twin))
     a2 = send(a, turn(-1))
-    b_twin = send(a, twins)
     b2 = send(b, turn(1))
+    late_a, twin = lax.optimization_barrier((a, twin))
+    b_twin = send(late_a, twins)
     a_twin = send(b, twins)
     half = (capacity + LABEL_ROWS) // 32 * 16
-    b2_twin = [send(a2[:half], twins), send(a2[half:], twins)]
-
+    b2_twin = send(a2[:half], twins), send(a2[half:], twins)
+    told = shape((1, (capacity // 128 + 1) * 128), F32)
+    a2_best = call(
+        functools.partial(middle_kernel, capacity), line, [VMEM] * 5, 4 * product, 5 * block_bytes
+    )(a2, block, twin, b, b_twin)
+    to_a2 = call(
+        functools.partial(a2_kernel, capacity), told, [VMEM] * 8, product, 2 * block_bytes
+    )(a2_best, a2, block, twin, b, b_twin, *b2_twin)
+    to_b2 = call(
+        functools.partial(b2_kernel, capacity), told, [VMEM] * 7, 5 * product, 6 * block_bytes
+    )(to_a2, b2, block, twin, a, a_twin, a2)
     near, column = call(
         functools.partial(near_kernel, capacity),
         (line, shape((slots, lanes), I32)),
@@ -215,13 +236,6 @@
         6 * product,
         6 * block_bytes,
     )(block, twin, a, a_twin, b, b_twin, position)
-    told = shape((1, (capacity // 128 + 1) * 128), F32)
-    def report(*refs):
-        kernel = functools.partial(report_kernel, capacity)
-        return call(kernel, told, [VMEM] * len(refs), 5 * product, 6 * block_bytes)(*refs)
-
-    to_a2 = report(a2, jnp.zeros(told.shape, F32), block, twin, b, b_twin, *b2_twin)
-    to_b2 = report(b2, to_a2, block, twin, a, a_twin, a2)
     told_a = send(to_a2, turn(2))
     told_b = send(to_b2, turn(-2))
     answers = call(
@@ -256,7 +270,7 @@
         2 * docs * width + 2 * groups * tall * lanes,
     )(offset, embeddings, labels.reshape(1, docs))
     received = lax.all_to_all(outgoing, "wide", split_axis=0, concat_axis=0, tiled=True)
-    quick, over = nearest(received, slot, 336)
+    quick, over = nearest(received, slot, 320)
     result = lax.cond(
         over[0, 0] > 0,
         lambda rows, places, unused: nearest(rows, places, groups * CAP)[0],

time: 120 us -> 118 us (0.983)
  waiting for transfers between devices: 26.6 us -> 24.2 us
    ppermute x11, waiting for transfers between devices: 16.9 us -> 14.5 us  [send(): return lax.ppermute(rows, 'narrow', pairs)]
    pallas_call x2 -> x3, Pallas kernels: 4.83 us -> 4.69 us  [the longest x1 2.24 us: nearest(): call(functools.partial(b2_kernel, capacity), told, [VMEM] * 7, 5 * produc...]
  transfers between devices with their start and end apart: 12 -> 12, of which waited for: 6 -> 5; matrix products, arithmetic and copies ran while one was open for 0% -> 0% of each run, Pallas kernels for 6% -> 6%
where the time goes in v4:
time: 118 us; the launch traced here: 117 us
  blocking collectives  44.7 us (38%)
  starting transfers between devices  35.1 us (30%)
  waiting for transfers between devices  24.2 us (21%)
  Pallas kernels  10.7 us (9%)
  local copies, waits for them, and re-layouts  1.77 us (2%)
    all_to_all x1, blocking collectives, shards(): lax.all_to_all(outgoing, 'wide', split_axis=0, concat_axis=0, tiled=True)  44.7 us
    ppermute x11, starting transfers between devices, send(): return lax.ppermute(rows, 'narrow', pairs)  31.3 us
    ppermute x11, waiting for transfers between devices, send(): return lax.ppermute(rows, 'narrow', pairs)  14.5 us
    all_to_all x1, waiting for transfers between devices, nearest(): lax.all_to_all(answers, 'wide', split_axis=0, concat_axis=0, tiled=True)  9.79 us
    all_to_all x1, starting transfers between devices, nearest(): lax.all_to_all(answers, 'wide', split_axis=0, concat_axis=0, tiled=True)  3.8 us
    pallas_call x1, Pallas kernels, nearest(): call(functools.partial(near_kernel, capacity), (line, shape((slots, lanes...  2.65 us
  transfers between devices with their start and end apart: 12, of which 5 were waited for; matrix products, arithmetic and copies ran while one was open for 0% of the time, Pallas kernels for 6%

profile of v4, /device:TPU:8, one launch (start us, length us, event | category | flops | bytes accessed | tf_op | source)
XLA Modules:
  0.0 117.0 jit_solution(14011764385263701705)
XLA Ops:
  0.0 1.0 copy-done
  1.0 0.7 copy-done.1
  1.7 0.7 shard_map.30
  2.4 44.7 %all_to_all.25.in_ref = bf16[32,136,128]{2,1,0:T(8,128)(2,1)S(1)} all-to-all(bf16[32,136,128]{2,1,0:T(8,128)(2,1)S(1)} %get-tuple-element.35), channel_id=1, replica_groups=mesh['wide'=32,'narrow'=16] {'wide'}, dimensions={0} | all-to-all | bytes 2228224 | tf_op jit(solution)/shard_map/all_to_all | solution.py:272
  47.1 1.0 shard_map.31
  48.1 2.4 %collective-permute-start.11 = (bf16[336,1024]{1,0:T(8,128)(2,1)S(1)}, bf16[336,1024]{1,0:T(8,128)(2,1)S(1)}, u32[]{:S(2)}, u32[]{:S(2)}) collective-permute-start(bf16[336,1024]{1,0:T(8,128)(2,1)S(1)} %get-tuple-element.36.own_ref), channel_id=1, source_target_pairs={{0,14},{1,3},{2,0},{3,5},{4,2},{5,7},{6,4},{7,9},{8,6},{9,11},{10,... | collective-permute-start | bytes 2064392 | tf_op jit(solution)/shard_map/ppermute | solution.py:209
  50.5 1.9 %collective-permute-start.12 = (bf16[336,1024]{1,0:T(8,128)(2,1)S(1)}, bf16[336,1024]{1,0:T(8,128)(2,1)S(1)}, u32[]{:S(2)}, u32[]{:S(2)}) collective-permute-start(bf16[336,1024]{1,0:T(8,128)(2,1)S(1)} %get-tuple-element.36.own_ref), channel_id=1, source_target_pairs={{0,1},{1,0},{2,3},{3,2},{4,5},{5,4},{6,7},{7,6},{8,9},{9,8},{10,11... | collective-permute-start | bytes 2064392 | tf_op jit(solution)/shard_map/ppermute | solution.py:209
  52.4 3.5 %collective-permute-start.13 = (bf16[336,1024]{1,0:T(8,128)(2,1)S(1)}, bf16[336,1024]{1,0:T(8,128)(2,1)S(1)}, u32[]{:S(2)}, u32[]{:S(2)}) collective-permute-start(bf16[336,1024]{1,0:T(8,128)(2,1)S(1)} %get-tuple-element.36.own_ref), channel_id=1, source_target_pairs={{0,2},{1,15},{2,4},{3,1},{4,6},{5,3},{6,8},{7,5},{8,10},{9,7},{10,... | collective-permute-start | bytes 2064392 | tf_op jit(solution)/shard_map/ppermute | solution.py:209
  55.9 8.5 %collective-permute-done.11.a_ref = bf16[336,1024]{1,0:T(8,128)(2,1)S(1)} collective-permute-done((bf16[336,1024]{1,0:T(8,128)(2,1)S(1)}, bf16[336,1024]{1,0:T(8,128)(2,1)S(1)}, u32[]{:S(2)}, u32[]{:S(2)}) %collective-permute-start.11) | collective-permute-done | bytes 688160 | tf_op jit(solution)/shard_map/ppermute | solution.py:209
  64.4 2.4 %collective-permute-start.16 = (bf16[336,1024]{1,0:T(8,128)(2,1)S(1)}, bf16[336,1024]{1,0:T(8,128)(2,1)S(1)}, u32[]{:S(2)}, u32[]{:S(2)}) collective-permute-start(bf16[336,1024]{1,0:T(8,128)(2,1)S(1)} %collective-permute-done.11.a_ref), channel_id=1, source_target_pairs={{0,14},{1,3},{2,0},{3,5},{4,2},{5,7},{6,4},{7,9},{8,6},{9,11},{10,... | collective-permute-start | bytes 2064392 | tf_op jit(solution)/shard_map/ppermute | solution.py:209
  66.9 0.0 collective-permute-done.12.twin_ref
  66.9 1.9 %collective-permute-start.15 = (bf16[336,1024]{1,0:T(8,128)(2,1)S(1)}, bf16[336,1024]{1,0:T(8,128)(2,1)S(1)}, u32[]{:S(2)}, u32[]{:S(2)}) collective-permute-start(bf16[336,1024]{1,0:T(8,128)(2,1)S(1)} %collective-permute-done.11.a_ref), channel_id=1, source_target_pairs={{0,1},{1,0},{2,3},{3,2},{4,5},{5,4},{6,7},{7,6},{8,9},{9,8},{10,11... | collective-permute-start | bytes 2064392 | tf_op jit(solution)/shard_map/ppermute | solution.py:209
  68.8 1.5 %collective-permute-done.13.b_ref = bf16[336,1024]{1,0:T(8,128)(2,1)S(1)} collective-permute-done((bf16[336,1024]{1,0:T(8,128)(2,1)S(1)}, bf16[336,1024]{1,0:T(8,128)(2,1)S(1)}, u32[]{:S(2)}, u32[]{:S(2)}) %collective-permute-start.13) | collective-permute-done | bytes 688160 | tf_op jit(solution)/shard_map/ppermute | solution.py:209
  70.3 1.9 %collective-permute-start.14 = (bf16[336,1024]{1,0:T(8,128)(2,1)S(1)}, bf16[336,1024]{1,0:T(8,128)(2,1)S(1)}, u32[]{:S(2)}, u32[]{:S(2)}) collective-permute-start(bf16[336,1024]{1,0:T(8,128)(2,1)S(1)} %collective-permute-done.13.b_ref), channel_id=1, source_target_pairs={{0,1},{1,0},{2,3},{3,2},{4,5},{5,4},{6,7},{7,6},{8,9},{9,8},{10,11... | collective-permute-start | bytes 2064392 | tf_op jit(solution)/shard_map/ppermute | solution.py:209
  72.2 2.4 %collective-permute-start.19 = (bf16[336,1024]{1,0:T(8,128)(2,1)S(1)}, bf16[336,1024]{1,0:T(8,128)(2,1)S(1)}, u32[]{:S(2)}, u32[]{:S(2)}) collective-permute-start(bf16[336,1024]{1,0:T(8,128)(2,1)S(1)} %collective-permute-done.13.b_ref), channel_id=1, source_target_pairs={{0,2},{1,15},{2,4},{3,1},{4,6},{5,3},{6,8},{7,5},{8,10},{9,7},{10,... | collective-permute-start | bytes 2064392 | tf_op jit(solution)/shard_map/ppermute | solution.py:209
  74.6 2.6 %collective-permute-done.16.a2_ref = bf16[336,1024]{1,0:T(8,128)(2,1)S(1)} collective-permute-done((bf16[336,1024]{1,0:T(8,128)(2,1)S(1)}, bf16[336,1024]{1,0:T(8,128)(2,1)S(1)}, u32[]{:S(2)}, u32[]{:S(2)}) %collective-permute-start.16) | collective-permute-done | bytes 688160 | tf_op jit(solution)/shard_map/ppermute | solution.py:209
  77.3 2.6 %collective-permute-start.18 = (bf16[176,1024]{1,0:T(8,128)(2,1)S(1)}, bf16[176,1024]{1,0:T(8,128)(2,1)S(1)}, u32[]{:S(2)}, u32[]{:S(2)}) collective-permute-start(bf16[176,1024]{1,0:T(8,128)(2,1)S(1)} %slice.21), channel_id=1, source_target_pairs={{0,1},{1,0},{2,3},{3,2},{4,5},{5,4},{6,7},{7,6},{8,9},{9,8},{10,11... | collective-permute-start | bytes 1081352 | tf_op jit(solution)/shard_map/ppermute | solution.py:209
  79.9 1.9 %collective-permute-start.17 = (bf16[160,1024]{1,0:T(8,128)(2,1)S(1)}, bf16[160,1024]{1,0:T(8,128)(2,1)S(1)}, u32[]{:S(2)}, u32[]{:S(2)}) collective-permute-start(bf16[160,1024]{1,0:T(8,128)(2,1)S(1)} %slice.20), channel_id=1, source_target_pairs={{0,1},{1,0},{2,3},{3,2},{4,5},{5,4},{6,7},{7,6},{8,9},{9,8},{10,11... | collective-permute-start | bytes 983048 | tf_op jit(solution)/shard_map/ppermute | solution.py:209
  81.8 1.8 %shard_map.33.a2_best = f32[1,320]{1,0:T(1,128)S(1)} custom-call(bf16[336,1024]{1,0:T(8,128)(2,1)S(1)} %collective-permute-done.16.a2_ref, bf16[336,1024]{1,0:T(8,128)(2,1)S(1)} %get-tuple-element.36.own_ref, bf16[336,1024]{1,0:T(8,128)(2,1)S(1)} %collective-permute-done.12.twin_ref, bf16[336,1024]{1,0:T(8,128)(2,1)S(1)} %collective-permute-done.13.b_ref, ...), custom_call_target="tpu_custom_call" | custom-call | flops 943718400 | bytes 3440640 | tf_op jit(solution)/shard_map/pallas_call | solution.py:223
  83.6 0.0 collective-permute-done.18.twin_1
  83.7 0.6 shard_map.34.seen_ref
  84.3 8.4 %collective-permute-start.20 = (f32[1,384]{1,0:T(1,128)S(1)}, f32[1,384]{1,0:T(1,128)S(1)}, u32[]{:S(2)}, u32[]{:S(2)}) collective-permute-start(f32[1,384]{1,0:T(1,128)S(1)} %shard_map.34.seen_ref), channel_id=1, source_target_pairs={{0,4},{1,13},{2,6},{3,15},{4,8},{5,1},{6,10},{7,3},{8,12},{9,5},{1... | collective-permute-start | bytes 4616 | tf_op jit(solution)/shard_map/ppermute | solution.py:209
  92.7 0.0 collective-permute-done.14.a_twin_ref
  92.7 2.2 %shard_map.35.seen_ref = f32[1,384]{1,0:T(1,128)S(1)} custom-call(f32[1,384]{1,0:T(1,128)S(1)} %shard_map.34.seen_ref, bf16[336,1024]{1,0:T(8,128)(2,1)S(1)} %collective-permute-done.19.b2_ref, bf16[336,1024]{1,0:T(8,128)(2,1)S(1)} %get-tuple-element.36.own_ref, bf16[336,1024]{1,0:T(8,128)(2,1)S(1)} %collective-permute-done.12.twin_ref, ...), custom_call_target="tpu_custom_call" | custom-call | flops 1179648000 | bytes 4128768 | tf_op jit(solution)/shard_map/pallas_call | solution.py:229
  95.0 1.9 %collective-permute-start.21 = (f32[1,384]{1,0:T(1,128)S(1)}, f32[1,384]{1,0:T(1,128)S(1)}, u32[]{:S(2)}, u32[]{:S(2)}) collective-permute-start(f32[1,384]{1,0:T(1,128)S(1)} %shard_map.35.seen_ref), channel_id=1, source_target_pairs={{0,12},{1,5},{2,14},{3,7},{4,0},{5,9},{6,2},{7,11},{8,4},{9,13},{1... | collective-permute-start | bytes 4616 | tf_op jit(solution)/shard_map/ppermute | solution.py:209
  96.9 2.7 %shard_map.32 = (f32[1,320]{1,0:T(1,128)S(1)}, s32[512,128]{1,0:T(8,128)S(1)}) custom-call(bf16[336,1024]{1,0:T(8,128)(2,1)S(1)} %get-tuple-element.36.own_ref, bf16[336,1024]{1,0:T(8,128)(2,1)S(1)} %collective-permute-done.12.twin_ref, bf16[336,1024]{1,0:T(8,128)(2,1)S(1)} %collective-permute-done.11.a_ref, ...), custom_call_target="tpu_custom_call" | custom-call | flops 1415577600 | bytes 4128768 | tf_op jit(solution)/shard_map/pallas_call | solution.py:232
  99.6 1.8 %collective-permute-done.21.told_b = f32[1,384]{1,0:T(1,128)S(1)} collective-permute-done((f32[1,384]{1,0:T(1,128)S(1)}, f32[1,384]{1,0:T(1,128)S(1)}, u32[]{:S(2)}, u32[]{:S(2)}) %collective-permute-start.21) | collective-permute-done | bytes 1568 | tf_op jit(solution)/shard_map/ppermute | solution.py:209
  101.4 0.9 shard_map.36
  102.2 3.8 %all-to-all-start.2 = ((f32[32,1,128]{2,1,0:T(1,128)}), f32[32,1,128]{2,1,0:T(1,128)S(1)}, u32[]{:S(2)}, u32[]{:S(2)}) async-start(f32[32,1,128]{2,1,0:T(1,128)} %bitcast.9), calls=%async_computation.2 | async-start | bytes 32768 | tf_op jit(solution)/shard_map/all_to_all | solution.py:248
  106.1 9.8 %all-to-all-done.2 = f32[32,1,128]{2,1,0:T(1,128)S(1)} async-done(((f32[32,1,128]{2,1,0:T(1,128)}), f32[32,1,128]{2,1,0:T(1,128)S(1)}, u32[]{:S(2)}, u32[]{:S(2)}) %all-to-all-start.2) | async-done | bytes 16416 | tf_op jit(solution)/shard_map/all_to_all | solution.py:248
  115.8 0.8 shard_map.37
  116.6 0.2 conditional.1
  (8 shorter events, 0.1 us)
Async XLA Ops:
  0.0 1.0 copy-start
  1.0 0.7 copy-start.1
  48.1 16.3 %collective-permute-start.11 = (bf16[336,1024]{1,0:T(8,128)(2,1)S(1)}, bf16[336,1024]{1,0:T(8,128)(2,1)S(1)}, u32[]{:S(2)}, u32[]{:S(2)}) collective-permute-start(bf16[336,1024]{1,0:T(8,128)(2,1)S(1)} %get-tuple-element.36.own_ref), channel_id=1, source_target_pairs={{0,14},{1,3},{2,0},{3,5},{4,2},{5,7},{6,4},{7,9},{8,6},{9,11},{10,... | collective-permute-start | bytes 2064392 | tf_op jit(solution)/shard_map/ppermute | solution.py:209
  50.5 16.4 %collective-permute-start.12 = (bf16[336,1024]{1,0:T(8,128)(2,1)S(1)}, bf16[336,1024]{1,0:T(8,128)(2,1)S(1)}, u32[]{:S(2)}, u32[]{:S(2)}) collective-permute-start(bf16[336,1024]{1,0:T(8,128)(2,1)S(1)} %get-tuple-element.36.own_ref), channel_id=1, source_target_pairs={{0,1},{1,0},{2,3},{3,2},{4,5},{5,4},{6,7},{7,6},{8,9},{9,8},{10,11... | collective-permute-start | bytes 2064392 | tf_op jit(solution)/shard_map/ppermute | solution.py:209
  52.4 17.9 %collective-permute-start.13 = (bf16[336,1024]{1,0:T(8,128)(2,1)S(1)}, bf16[336,1024]{1,0:T(8,128)(2,1)S(1)}, u32[]{:S(2)}, u32[]{:S(2)}) collective-permute-start(bf16[336,1024]{1,0:T(8,128)(2,1)S(1)} %get-tuple-element.36.own_ref), channel_id=1, source_target_pairs={{0,2},{1,15},{2,4},{3,1},{4,6},{5,3},{6,8},{7,5},{8,10},{9,7},{10,... | collective-permute-start | bytes 2064392 | tf_op jit(solution)/shard_map/ppermute | solution.py:209
  64.4 12.8 %collective-permute-start.16 = (bf16[336,1024]{1,0:T(8,128)(2,1)S(1)}, bf16[336,1024]{1,0:T(8,128)(2,1)S(1)}, u32[]{:S(2)}, u32[]{:S(2)}) collective-permute-start(bf16[336,1024]{1,0:T(8,128)(2,1)S(1)} %collective-permute-done.11.a_ref), channel_id=1, source_target_pairs={{0,14},{1,3},{2,0},{3,5},{4,2},{5,7},{6,4},{7,9},{8,6},{9,11},{10,... | collective-permute-start | bytes 2064392 | tf_op jit(solution)/shard_map/ppermute | solution.py:209
  66.9 14.9 %collective-permute-start.15 = (bf16[336,1024]{1,0:T(8,128)(2,1)S(1)}, bf16[336,1024]{1,0:T(8,128)(2,1)S(1)}, u32[]{:S(2)}, u32[]{:S(2)}) collective-permute-start(bf16[336,1024]{1,0:T(8,128)(2,1)S(1)} %collective-permute-done.11.a_ref), channel_id=1, source_target_pairs={{0,1},{1,0},{2,3},{3,2},{4,5},{5,4},{6,7},{7,6},{8,9},{9,8},{10,11... | collective-permute-start | bytes 2064392 | tf_op jit(solution)/shard_map/ppermute | solution.py:209
  70.3 22.4 %collective-permute-start.14 = (bf16[336,1024]{1,0:T(8,128)(2,1)S(1)}, bf16[336,1024]{1,0:T(8,128)(2,1)S(1)}, u32[]{:S(2)}, u32[]{:S(2)}) collective-permute-start(bf16[336,1024]{1,0:T(8,128)(2,1)S(1)} %collective-permute-done.13.b_ref), channel_id=1, source_target_pairs={{0,1},{1,0},{2,3},{3,2},{4,5},{5,4},{6,7},{7,6},{8,9},{9,8},{10,11... | collective-permute-start | bytes 2064392 | tf_op jit(solution)/shard_map/ppermute | solution.py:209
  72.2 20.5 %collective-permute-start.19 = (bf16[336,1024]{1,0:T(8,128)(2,1)S(1)}, bf16[336,1024]{1,0:T(8,128)(2,1)S(1)}, u32[]{:S(2)}, u32[]{:S(2)}) collective-permute-start(bf16[336,1024]{1,0:T(8,128)(2,1)S(1)} %collective-permute-done.13.b_ref), channel_id=1, source_target_pairs={{0,2},{1,15},{2,4},{3,1},{4,6},{5,3},{6,8},{7,5},{8,10},{9,7},{10,... | collective-permute-start | bytes 2064392 | tf_op jit(solution)/shard_map/ppermute | solution.py:209
  77.3 6.4 %collective-permute-start.18 = (bf16[176,1024]{1,0:T(8,128)(2,1)S(1)}, bf16[176,1024]{1,0:T(8,128)(2,1)S(1)}, u32[]{:S(2)}, u32[]{:S(2)}) collective-permute-start(bf16[176,1024]{1,0:T(8,128)(2,1)S(1)} %slice.21), channel_id=1, source_target_pairs={{0,1},{1,0},{2,3},{3,2},{4,5},{5,4},{6,7},{7,6},{8,9},{9,8},{10,11... | collective-permute-start | bytes 1081352 | tf_op jit(solution)/shard_map/ppermute | solution.py:209
  79.9 3.8 %collective-permute-start.17 = (bf16[160,1024]{1,0:T(8,128)(2,1)S(1)}, bf16[160,1024]{1,0:T(8,128)(2,1)S(1)}, u32[]{:S(2)}, u32[]{:S(2)}) collective-permute-start(bf16[160,1024]{1,0:T(8,128)(2,1)S(1)} %slice.20), channel_id=1, source_target_pairs={{0,1},{1,0},{2,3},{3,2},{4,5},{5,4},{6,7},{7,6},{8,9},{9,8},{10,11... | collective-permute-start | bytes 983048 | tf_op jit(solution)/shard_map/ppermute | solution.py:209
  84.3 17.1 %collective-permute-start.20 = (f32[1,384]{1,0:T(1,128)S(1)}, f32[1,384]{1,0:T(1,128)S(1)}, u32[]{:S(2)}, u32[]{:S(2)}) collective-permute-start(f32[1,384]{1,0:T(1,128)S(1)} %shard_map.34.seen_ref), channel_id=1, source_target_pairs={{0,4},{1,13},{2,6},{3,15},{4,8},{5,1},{6,10},{7,3},{8,12},{9,5},{1... | collective-permute-start | bytes 4616 | tf_op jit(solution)/shard_map/ppermute | solution.py:209
  95.0 6.4 %collective-permute-start.21 = (f32[1,384]{1,0:T(1,128)S(1)}, f32[1,384]{1,0:T(1,128)S(1)}, u32[]{:S(2)}, u32[]{:S(2)}) collective-permute-start(f32[1,384]{1,0:T(1,128)S(1)} %shard_map.35.seen_ref), channel_id=1, source_target_pairs={{0,12},{1,5},{2,14},{3,7},{4,0},{5,9},{6,2},{7,11},{8,4},{9,13},{1... | collective-permute-start | bytes 4616 | tf_op jit(solution)/shard_map/ppermute | solution.py:209
  102.2 13.6 %all-to-all-start.2 = ((f32[32,1,128]{2,1,0:T(1,128)}), f32[32,1,128]{2,1,0:T(1,128)S(1)}, u32[]{:S(2)}, u32[]{:S(2)}) async-start(f32[32,1,128]{2,1,0:T(1,128)} %bitcast.9), calls=%async_computation.2 | async-start | bytes 32768 | tf_op jit(solution)/shard_map/all_to_all | solution.py:248

commit v5 on v4

--- a/solution.py
+++ b/solution.py
@@ -11,7 +11,7 @@
 CL_GROUP = 4
 CAP = 16
 LIFT = 4.0
-LABEL_ROWS = 16
+LABEL_ROWS = 8
 F32, BF16, I32 = jnp.float32, jnp.bfloat16, jnp.int32
 NT = (((1,), (1,)), ((), ()))
 NN = (((1,), (0,)), ((), ()))
@@ -96,9 +96,8 @@
         part = in_ref[:, k * CAP : (k + 1) * CAP, :].reshape(slots, lanes)
         out_ref[:capacity, k * lanes : (k + 1) * lanes] = dot(pick, part, NN).astype(BF16)
     marks = dot(labels.astype(BF16), pick, NT).astype(BF16)
-    marks = jnp.concatenate([marks, jnp.zeros((below, width - capacity), BF16)], axis=1)
-    flag = jnp.concatenate([jnp.zeros((below, width - lanes), F32), over], axis=1).astype(BF16)
-    out_ref[capacity:, :] = jnp.concatenate([marks, flag], axis=0)
+    gap = jnp.zeros((below, width - lanes - capacity), BF16)
+    out_ref[capacity:, :] = jnp.concatenate([marks, gap, over.astype(BF16)], axis=1)
 
 
 def best_of(ref, others, capacity, skip_self=False):

time: 118 us -> 117 us (level)
  no operation moved by 1% of the time
where the time goes in v5:
time: 117 us; the launch traced here: 116 us
  blocking collectives  44.7 us (38%)
  starting transfers between devices  34.7 us (30%)
  waiting for transfers between devices  23.9 us (20%)
  Pallas kernels  10.7 us (9%)
  local copies, waits for them, and re-layouts  1.77 us (2%)
    all_to_all x1, blocking collectives, shards(): lax.all_to_all(outgoing, 'wide', split_axis=0, concat_axis=0, tiled=True)  44.7 us
    ppermute x11, starting transfers between devices, send(): return lax.ppermute(rows, 'narrow', pairs)  30.9 us
    ppermute x11, waiting for transfers between devices, send(): return lax.ppermute(rows, 'narrow', pairs)  14.1 us
    all_to_all x1, waiting for transfers between devices, nearest(): lax.all_to_all(answers, 'wide', split_axis=0, concat_axis=0, tiled=True)  9.79 us
    all_to_all x1, starting transfers between devices, nearest(): lax.all_to_all(answers, 'wide', split_axis=0, concat_axis=0, tiled=True)  3.8 us
    pallas_call x1, Pallas kernels, nearest(): call(functools.partial(near_kernel, capacity), (line, shape((slots, lanes...  2.66 us
  transfers between devices with their start and end apart: 12, of which 5 were waited for; matrix products, arithmetic and copies ran while one was open for 0% of the time, Pallas kernels for 6%

profile of v5, /device:TPU:8, one launch (start us, length us, event | category | flops | bytes accessed | tf_op | source)
XLA Modules:
  0.0 116.3 jit_solution(16329005408067926515)
XLA Ops:
  0.0 1.0 copy-done
  1.0 0.7 copy-done.1
  1.7 0.7 shard_map.30
  2.4 44.7 %all_to_all.25.in_ref = bf16[32,136,128]{2,1,0:T(8,128)(2,1)S(1)} all-to-all(bf16[32,136,128]{2,1,0:T(8,128)(2,1)S(1)} %get-tuple-element.35), channel_id=1, replica_groups=mesh['wide'=32,'narrow'=16] {'wide'}, dimensions={0} | all-to-all | bytes 2228224 | tf_op jit(solution)/shard_map/all_to_all | solution.py:271
  47.1 1.0 shard_map.31
  48.1 2.4 %collective-permute-start.11 = (bf16[328,1024]{1,0:T(8,128)(2,1)S(1)}, bf16[328,1024]{1,0:T(8,128)(2,1)S(1)}, u32[]{:S(2)}, u32[]{:S(2)}) collective-permute-start(bf16[328,1024]{1,0:T(8,128)(2,1)S(1)} %get-tuple-element.36.own_ref), channel_id=1, source_target_pairs={{0,14},{1,3},{2,0},{3,5},{4,2},{5,7},{6,4},{7,9},{8,6},{9,11},{10,... | collective-permute-start | bytes 2015240 | tf_op jit(solution)/shard_map/ppermute | solution.py:208
  50.5 1.9 %collective-permute-start.12 = (bf16[328,1024]{1,0:T(8,128)(2,1)S(1)}, bf16[328,1024]{1,0:T(8,128)(2,1)S(1)}, u32[]{:S(2)}, u32[]{:S(2)}) collective-permute-start(bf16[328,1024]{1,0:T(8,128)(2,1)S(1)} %get-tuple-element.36.own_ref), channel_id=1, source_target_pairs={{0,1},{1,0},{2,3},{3,2},{4,5},{5,4},{6,7},{7,6},{8,9},{9,8},{10,11... | collective-permute-start | bytes 2015240 | tf_op jit(solution)/shard_map/ppermute | solution.py:208
  52.4 3.5 %collective-permute-start.13 = (bf16[328,1024]{1,0:T(8,128)(2,1)S(1)}, bf16[328,1024]{1,0:T(8,128)(2,1)S(1)}, u32[]{:S(2)}, u32[]{:S(2)}) collective-permute-start(bf16[328,1024]{1,0:T(8,128)(2,1)S(1)} %get-tuple-element.36.own_ref), channel_id=1, source_target_pairs={{0,2},{1,15},{2,4},{3,1},{4,6},{5,3},{6,8},{7,5},{8,10},{9,7},{10,... | collective-permute-start | bytes 2015240 | tf_op jit(solution)/shard_map/ppermute | solution.py:208
  55.9 8.2 %collective-permute-done.11.a_ref = bf16[328,1024]{1,0:T(8,128)(2,1)S(1)} collective-permute-done((bf16[328,1024]{1,0:T(8,128)(2,1)S(1)}, bf16[328,1024]{1,0:T(8,128)(2,1)S(1)}, u32[]{:S(2)}, u32[]{:S(2)}) %collective-permute-start.11) | collective-permute-done | bytes 671776 | tf_op jit(solution)/shard_map/ppermute | solution.py:208
  64.1 2.4 %collective-permute-start.16 = (bf16[328,1024]{1,0:T(8,128)(2,1)S(1)}, bf16[328,1024]{1,0:T(8,128)(2,1)S(1)}, u32[]{:S(2)}, u32[]{:S(2)}) collective-permute-start(bf16[328,1024]{1,0:T(8,128)(2,1)S(1)} %collective-permute-done.11.a_ref), channel_id=1, source_target_pairs={{0,14},{1,3},{2,0},{3,5},{4,2},{5,7},{6,4},{7,9},{8,6},{9,11},{10,... | collective-permute-start | bytes 2015240 | tf_op jit(solution)/shard_map/ppermute | solution.py:208
  66.5 0.0 collective-permute-done.12.twin_ref
  66.5 1.9 %collective-permute-start.15 = (bf16[328,1024]{1,0:T(8,128)(2,1)S(1)}, bf16[328,1024]{1,0:T(8,128)(2,1)S(1)}, u32[]{:S(2)}, u32[]{:S(2)}) collective-permute-start(bf16[328,1024]{1,0:T(8,128)(2,1)S(1)} %collective-permute-done.11.a_ref), channel_id=1, source_target_pairs={{0,1},{1,0},{2,3},{3,2},{4,5},{5,4},{6,7},{7,6},{8,9},{9,8},{10,11... | collective-permute-start | bytes 2015240 | tf_op jit(solution)/shard_map/ppermute | solution.py:208
  68.4 1.7 %collective-permute-done.13.b_ref = bf16[328,1024]{1,0:T(8,128)(2,1)S(1)} collective-permute-done((bf16[328,1024]{1,0:T(8,128)(2,1)S(1)}, bf16[328,1024]{1,0:T(8,128)(2,1)S(1)}, u32[]{:S(2)}, u32[]{:S(2)}) %collective-permute-start.13) | collective-permute-done | bytes 671776 | tf_op jit(solution)/shard_map/ppermute | solution.py:208
  70.1 1.9 %collective-permute-start.14 = (bf16[328,1024]{1,0:T(8,128)(2,1)S(1)}, bf16[328,1024]{1,0:T(8,128)(2,1)S(1)}, u32[]{:S(2)}, u32[]{:S(2)}) collective-permute-start(bf16[328,1024]{1,0:T(8,128)(2,1)S(1)} %collective-permute-done.13.b_ref), channel_id=1, source_target_pairs={{0,1},{1,0},{2,3},{3,2},{4,5},{5,4},{6,7},{7,6},{8,9},{9,8},{10,11... | collective-permute-start | bytes 2015240 | tf_op jit(solution)/shard_map/ppermute | solution.py:208
  72.1 2.2 %collective-permute-start.19 = (bf16[328,1024]{1,0:T(8,128)(2,1)S(1)}, bf16[328,1024]{1,0:T(8,128)(2,1)S(1)}, u32[]{:S(2)}, u32[]{:S(2)}) collective-permute-start(bf16[328,1024]{1,0:T(8,128)(2,1)S(1)} %collective-permute-done.13.b_ref), channel_id=1, source_target_pairs={{0,2},{1,15},{2,4},{3,1},{4,6},{5,3},{6,8},{7,5},{8,10},{9,7},{10,... | collective-permute-start | bytes 2015240 | tf_op jit(solution)/shard_map/ppermute | solution.py:208
  74.3 2.4 %collective-permute-done.16.a2_ref = bf16[328,1024]{1,0:T(8,128)(2,1)S(1)} collective-permute-done((bf16[328,1024]{1,0:T(8,128)(2,1)S(1)}, bf16[328,1024]{1,0:T(8,128)(2,1)S(1)}, u32[]{:S(2)}, u32[]{:S(2)}) %collective-permute-start.16) | collective-permute-done | bytes 671776 | tf_op jit(solution)/shard_map/ppermute | solution.py:208
  76.7 2.9 %collective-permute-start.18 = (bf16[168,1024]{1,0:T(8,128)(2,1)S(1)}, bf16[168,1024]{1,0:T(8,128)(2,1)S(1)}, u32[]{:S(2)}, u32[]{:S(2)}) collective-permute-start(bf16[168,1024]{1,0:T(8,128)(2,1)S(1)} %slice.21), channel_id=1, source_target_pairs={{0,1},{1,0},{2,3},{3,2},{4,5},{5,4},{6,7},{7,6},{8,9},{9,8},{10,11... | collective-permute-start | bytes 1032200 | tf_op jit(solution)/shard_map/ppermute | solution.py:208
  79.7 1.9 %collective-permute-start.17 = (bf16[160,1024]{1,0:T(8,128)(2,1)S(1)}, bf16[160,1024]{1,0:T(8,128)(2,1)S(1)}, u32[]{:S(2)}, u32[]{:S(2)}) collective-permute-start(bf16[160,1024]{1,0:T(8,128)(2,1)S(1)} %slice.20), channel_id=1, source_target_pairs={{0,1},{1,0},{2,3},{3,2},{4,5},{5,4},{6,7},{7,6},{8,9},{9,8},{10,11... | collective-permute-start | bytes 983048 | tf_op jit(solution)/shard_map/ppermute | solution.py:208
  81.6 0.0 collective-permute-done.15.b_twin_ref
  81.6 1.8 %shard_map.33.a2_best = f32[1,320]{1,0:T(1,128)S(1)} custom-call(bf16[328,1024]{1,0:T(8,128)(2,1)S(1)} %collective-permute-done.16.a2_ref, bf16[328,1024]{1,0:T(8,128)(2,1)S(1)} %get-tuple-element.36.own_ref, bf16[328,1024]{1,0:T(8,128)(2,1)S(1)} %collective-permute-done.12.twin_ref, bf16[328,1024]{1,0:T(8,128)(2,1)S(1)} %collective-permute-done.13.b_ref, ...), custom_call_target="tpu_custom_call" | custom-call | flops 943718400 | bytes 3358720 | tf_op jit(solution)/shard_map/pallas_call | solution.py:222
  83.5 0.0 collective-permute-done.18.twin_1
  83.5 0.6 shard_map.34.seen_ref
  84.1 7.9 %collective-permute-start.20 = (f32[1,384]{1,0:T(1,128)S(1)}, f32[1,384]{1,0:T(1,128)S(1)}, u32[]{:S(2)}, u32[]{:S(2)}) collective-permute-start(f32[1,384]{1,0:T(1,128)S(1)} %shard_map.34.seen_ref), channel_id=1, source_target_pairs={{0,4},{1,13},{2,6},{3,15},{4,8},{5,1},{6,10},{7,3},{8,12},{9,5},{1... | collective-permute-start | bytes 4616 | tf_op jit(solution)/shard_map/ppermute | solution.py:208
  92.0 2.2 %shard_map.35.seen_ref = f32[1,384]{1,0:T(1,128)S(1)} custom-call(f32[1,384]{1,0:T(1,128)S(1)} %shard_map.34.seen_ref, bf16[328,1024]{1,0:T(8,128)(2,1)S(1)} %collective-permute-done.19.b2_ref, bf16[328,1024]{1,0:T(8,128)(2,1)S(1)} %get-tuple-element.36.own_ref, bf16[328,1024]{1,0:T(8,128)(2,1)S(1)} %collective-permute-done.12.twin_ref, ...), custom_call_target="tpu_custom_call" | custom-call | flops 1179648000 | bytes 4030464 | tf_op jit(solution)/shard_map/pallas_call | solution.py:228
  94.3 1.9 %collective-permute-start.21 = (f32[1,384]{1,0:T(1,128)S(1)}, f32[1,384]{1,0:T(1,128)S(1)}, u32[]{:S(2)}, u32[]{:S(2)}) collective-permute-start(f32[1,384]{1,0:T(1,128)S(1)} %shard_map.35.seen_ref), channel_id=1, source_target_pairs={{0,12},{1,5},{2,14},{3,7},{4,0},{5,9},{6,2},{7,11},{8,4},{9,13},{1... | collective-permute-start | bytes 4616 | tf_op jit(solution)/shard_map/ppermute | solution.py:208
  96.2 2.7 %shard_map.32 = (f32[1,320]{1,0:T(1,128)S(1)}, s32[512,128]{1,0:T(8,128)S(1)}) custom-call(bf16[328,1024]{1,0:T(8,128)(2,1)S(1)} %get-tuple-element.36.own_ref, bf16[328,1024]{1,0:T(8,128)(2,1)S(1)} %collective-permute-done.12.twin_ref, bf16[328,1024]{1,0:T(8,128)(2,1)S(1)} %collective-permute-done.11.a_ref, ...), custom_call_target="tpu_custom_call" | custom-call | flops 1415577600 | bytes 4030464 | tf_op jit(solution)/shard_map/pallas_call | solution.py:231
  98.9 1.8 %collective-permute-done.21.told_b = f32[1,384]{1,0:T(1,128)S(1)} collective-permute-done((f32[1,384]{1,0:T(1,128)S(1)}, f32[1,384]{1,0:T(1,128)S(1)}, u32[]{:S(2)}, u32[]{:S(2)}) %collective-permute-start.21) | collective-permute-done | bytes 1568 | tf_op jit(solution)/shard_map/ppermute | solution.py:208
  100.7 0.9 shard_map.36
  101.5 3.8 %all-to-all-start.2 = ((f32[32,1,128]{2,1,0:T(1,128)}), f32[32,1,128]{2,1,0:T(1,128)S(1)}, u32[]{:S(2)}, u32[]{:S(2)}) async-start(f32[32,1,128]{2,1,0:T(1,128)} %bitcast.9), calls=%async_computation.2 | async-start | bytes 32768 | tf_op jit(solution)/shard_map/all_to_all | solution.py:247
  105.4 9.8 %all-to-all-done.2 = f32[32,1,128]{2,1,0:T(1,128)S(1)} async-done(((f32[32,1,128]{2,1,0:T(1,128)}), f32[32,1,128]{2,1,0:T(1,128)S(1)}, u32[]{:S(2)}, u32[]{:S(2)}) %all-to-all-start.2) | async-done | bytes 16416 | tf_op jit(solution)/shard_map/all_to_all | solution.py:247
  115.1 0.8 shard_map.37
  115.9 0.2 conditional.1
  (8 shorter events, 0.1 us)
Async XLA Ops:
  0.0 1.0 copy-start
  1.0 0.7 copy-start.1
  48.1 16.0 %collective-permute-start.11 = (bf16[328,1024]{1,0:T(8,128)(2,1)S(1)}, bf16[328,1024]{1,0:T(8,128)(2,1)S(1)}, u32[]{:S(2)}, u32[]{:S(2)}) collective-permute-start(bf16[328,1024]{1,0:T(8,128)(2,1)S(1)} %get-tuple-element.36.own_ref), channel_id=1, source_target_pairs={{0,14},{1,3},{2,0},{3,5},{4,2},{5,7},{6,4},{7,9},{8,6},{9,11},{10,... | collective-permute-start | bytes 2015240 | tf_op jit(solution)/shard_map/ppermute | solution.py:208
  50.5 16.0 %collective-permute-start.12 = (bf16[328,1024]{1,0:T(8,128)(2,1)S(1)}, bf16[328,1024]{1,0:T(8,128)(2,1)S(1)}, u32[]{:S(2)}, u32[]{:S(2)}) collective-permute-start(bf16[328,1024]{1,0:T(8,128)(2,1)S(1)} %get-tuple-element.36.own_ref), channel_id=1, source_target_pairs={{0,1},{1,0},{2,3},{3,2},{4,5},{5,4},{6,7},{7,6},{8,9},{9,8},{10,11... | collective-permute-start | bytes 2015240 | tf_op jit(solution)/shard_map/ppermute | solution.py:208
  52.4 17.8 %collective-permute-start.13 = (bf16[328,1024]{1,0:T(8,128)(2,1)S(1)}, bf16[328,1024]{1,0:T(8,128)(2,1)S(1)}, u32[]{:S(2)}, u32[]{:S(2)}) collective-permute-start(bf16[328,1024]{1,0:T(8,128)(2,1)S(1)} %get-tuple-element.36.own_ref), channel_id=1, source_target_pairs={{0,2},{1,15},{2,4},{3,1},{4,6},{5,3},{6,8},{7,5},{8,10},{9,7},{10,... | collective-permute-start | bytes 2015240 | tf_op jit(solution)/shard_map/ppermute | solution.py:208
  64.1 12.6 %collective-permute-start.16 = (bf16[328,1024]{1,0:T(8,128)(2,1)S(1)}, bf16[328,1024]{1,0:T(8,128)(2,1)S(1)}, u32[]{:S(2)}, u32[]{:S(2)}) collective-permute-start(bf16[328,1024]{1,0:T(8,128)(2,1)S(1)} %collective-permute-done.11.a_ref), channel_id=1, source_target_pairs={{0,14},{1,3},{2,0},{3,5},{4,2},{5,7},{6,4},{7,9},{8,6},{9,11},{10,... | collective-permute-start | bytes 2015240 | tf_op jit(solution)/shard_map/ppermute | solution.py:208
  66.5 15.1 %collective-permute-start.15 = (bf16[328,1024]{1,0:T(8,128)(2,1)S(1)}, bf16[328,1024]{1,0:T(8,128)(2,1)S(1)}, u32[]{:S(2)}, u32[]{:S(2)}) collective-permute-start(bf16[328,1024]{1,0:T(8,128)(2,1)S(1)} %collective-permute-done.11.a_ref), channel_id=1, source_target_pairs={{0,1},{1,0},{2,3},{3,2},{4,5},{5,4},{6,7},{7,6},{8,9},{9,8},{10,11... | collective-permute-start | bytes 2015240 | tf_op jit(solution)/shard_map/ppermute | solution.py:208
  70.1 21.9 %collective-permute-start.14 = (bf16[328,1024]{1,0:T(8,128)(2,1)S(1)}, bf16[328,1024]{1,0:T(8,128)(2,1)S(1)}, u32[]{:S(2)}, u32[]{:S(2)}) collective-permute-start(bf16[328,1024]{1,0:T(8,128)(2,1)S(1)} %collective-permute-done.13.b_ref), channel_id=1, source_target_pairs={{0,1},{1,0},{2,3},{3,2},{4,5},{5,4},{6,7},{7,6},{8,9},{9,8},{10,11... | collective-permute-start | bytes 2015240 | tf_op jit(solution)/shard_map/ppermute | solution.py:208
  72.1 20.0 %collective-permute-start.19 = (bf16[328,1024]{1,0:T(8,128)(2,1)S(1)}, bf16[328,1024]{1,0:T(8,128)(2,1)S(1)}, u32[]{:S(2)}, u32[]{:S(2)}) collective-permute-start(bf16[328,1024]{1,0:T(8,128)(2,1)S(1)} %collective-permute-done.13.b_ref), channel_id=1, source_target_pairs={{0,2},{1,15},{2,4},{3,1},{4,6},{5,3},{6,8},{7,5},{8,10},{9,7},{10,... | collective-permute-start | bytes 2015240 | tf_op jit(solution)/shard_map/ppermute | solution.py:208
  76.7 6.7 %collective-permute-start.18 = (bf16[168,1024]{1,0:T(8,128)(2,1)S(1)}, bf16[168,1024]{1,0:T(8,128)(2,1)S(1)}, u32[]{:S(2)}, u32[]{:S(2)}) collective-permute-start(bf16[168,1024]{1,0:T(8,128)(2,1)S(1)} %slice.21), channel_id=1, source_target_pairs={{0,1},{1,0},{2,3},{3,2},{4,5},{5,4},{6,7},{7,6},{8,9},{9,8},{10,11... | collective-permute-start | bytes 1032200 | tf_op jit(solution)/shard_map/ppermute | solution.py:208
  79.7 3.8 %collective-permute-start.17 = (bf16[160,1024]{1,0:T(8,128)(2,1)S(1)}, bf16[160,1024]{1,0:T(8,128)(2,1)S(1)}, u32[]{:S(2)}, u32[]{:S(2)}) collective-permute-start(bf16[160,1024]{1,0:T(8,128)(2,1)S(1)} %slice.20), channel_id=1, source_target_pairs={{0,1},{1,0},{2,3},{3,2},{4,5},{5,4},{6,7},{7,6},{8,9},{9,8},{10,11... | collective-permute-start | bytes 983048 | tf_op jit(solution)/shard_map/ppermute | solution.py:208
  84.1 16.6 %collective-permute-start.20 = (f32[1,384]{1,0:T(1,128)S(1)}, f32[1,384]{1,0:T(1,128)S(1)}, u32[]{:S(2)}, u32[]{:S(2)}) collective-permute-start(f32[1,384]{1,0:T(1,128)S(1)} %shard_map.34.seen_ref), channel_id=1, source_target_pairs={{0,4},{1,13},{2,6},{3,15},{4,8},{5,1},{6,10},{7,3},{8,12},{9,5},{1... | collective-permute-start | bytes 4616 | tf_op jit(solution)/shard_map/ppermute | solution.py:208
  94.3 6.4 %collective-permute-start.21 = (f32[1,384]{1,0:T(1,128)S(1)}, f32[1,384]{1,0:T(1,128)S(1)}, u32[]{:S(2)}, u32[]{:S(2)}) collective-permute-start(f32[1,384]{1,0:T(1,128)S(1)} %shard_map.35.seen_ref), channel_id=1, source_target_pairs={{0,12},{1,5},{2,14},{3,7},{4,0},{5,9},{6,2},{7,11},{8,4},{9,13},{1... | collective-permute-start | bytes 4616 | tf_op jit(solution)/shard_map/ppermute | solution.py:208
  101.5 13.6 %all-to-all-start.2 = ((f32[32,1,128]{2,1,0:T(1,128)}), f32[32,1,128]{2,1,0:T(1,128)S(1)}, u32[]{:S(2)}, u32[]{:S(2)}) async-start(f32[32,1,128]{2,1,0:T(1,128)} %bitcast.9), calls=%async_computation.2 | async-start | bytes 32768 | tf_op jit(solution)/shard_map/all_to_all | solution.py:247

commit v6 on v5

--- a/solution.py
+++ b/solution.py
@@ -160,8 +160,13 @@
     told = jnp.maximum(told_a[...], told_b[...])
     over = jnp.maximum(told, seen_ref[...])[:, capacity : capacity + 1]
     best = jnp.maximum(jnp.maximum(near_ref[...], told[:, :capacity]) - LIFT, -1.0)
-    hit = iota((slots, capacity), 1) == position_ref[:, :1]
-    values = jnp.max(jnp.where(hit, best, -1.0), axis=1, keepdims=True)
+    wide = told.shape[1]
+    best = jnp.concatenate([best, jnp.full((1, wide - capacity), -1.0, F32)], axis=1)
+    values = jnp.full((slots, lanes), -1.0, F32)
+    for first in range(0, wide, lanes):
+        hit = iota((slots, lanes), 1) + first == position_ref[...]
+        values = jnp.maximum(values, jnp.where(hit, best[:, first : first + lanes], -1.0))
+    values = jnp.max(values, axis=1, keepdims=True)
     values = jnp.broadcast_to(values, (slots, lanes)).reshape(groups, CAP, lanes)
     same = iota((groups, CAP, lanes), 1) == iota((groups, CAP, lanes), 2)
     answers = jnp.max(jnp.where(same, values, -1.0), axis=1)

time: 117 us -> 117 us (level)
  no operation moved by 1% of the time
where the time goes in v6:
time: 117 us; the launch traced here: 116 us
  blocking collectives  44.7 us (38%)
  starting transfers between devices  34.7 us (30%)
  waiting for transfers between devices  23.9 us (20%)
  Pallas kernels  10.6 us (9%)
  local copies, waits for them, and re-layouts  1.77 us (2%)
    all_to_all x1, blocking collectives, shards(): lax.all_to_all(outgoing, 'wide', split_axis=0, concat_axis=0, tiled=True)  44.7 us
    ppermute x11, starting transfers between devices, send(): return lax.ppermute(rows, 'narrow', pairs)  30.9 us
    ppermute x11, waiting for transfers between devices, send(): return lax.ppermute(rows, 'narrow', pairs)  14.1 us
    all_to_all x1, waiting for transfers between devices, nearest(): lax.all_to_all(answers, 'wide', split_axis=0, concat_axis=0, tiled=True)  9.79 us
    all_to_all x1, starting transfers between devices, nearest(): lax.all_to_all(answers, 'wide', split_axis=0, concat_axis=0, tiled=True)  3.8 us
    pallas_call x1, Pallas kernels, nearest(): call(functools.partial(near_kernel, capacity), (line, shape((slots, lanes...  2.66 us
  transfers between devices with their start and end apart: 12, of which 5 were waited for; matrix products, arithmetic and copies ran while one was open for 0% of the time, Pallas kernels for 6%

profile of v6, /device:TPU:8, one launch (start us, length us, event | category | flops | bytes accessed | tf_op | source)
XLA Modules:
  0.0 116.3 jit_solution(4330546980560802857)
XLA Ops:
  0.0 1.0 copy-done
  1.0 0.7 copy-done.1
  1.7 0.7 shard_map.30
  2.4 44.7 %all_to_all.25.in_ref = bf16[32,136,128]{2,1,0:T(8,128)(2,1)S(1)} all-to-all(bf16[32,136,128]{2,1,0:T(8,128)(2,1)S(1)} %get-tuple-element.35), channel_id=1, replica_groups=mesh['wide'=32,'narrow'=16] {'wide'}, dimensions={0} | all-to-all | bytes 2228224 | tf_op jit(solution)/shard_map/all_to_all | solution.py:276
  47.1 1.0 shard_map.31
  48.1 2.4 %collective-permute-start.11 = (bf16[328,1024]{1,0:T(8,128)(2,1)S(1)}, bf16[328,1024]{1,0:T(8,128)(2,1)S(1)}, u32[]{:S(2)}, u32[]{:S(2)}) collective-permute-start(bf16[328,1024]{1,0:T(8,128)(2,1)S(1)} %get-tuple-element.36.own_ref), channel_id=1, source_target_pairs={{0,14},{1,3},{2,0},{3,5},{4,2},{5,7},{6,4},{7,9},{8,6},{9,11},{10,... | collective-permute-start | bytes 2015240 | tf_op jit(solution)/shard_map/ppermute | solution.py:213
  50.5 1.9 %collective-permute-start.12 = (bf16[328,1024]{1,0:T(8,128)(2,1)S(1)}, bf16[328,1024]{1,0:T(8,128)(2,1)S(1)}, u32[]{:S(2)}, u32[]{:S(2)}) collective-permute-start(bf16[328,1024]{1,0:T(8,128)(2,1)S(1)} %get-tuple-element.36.own_ref), channel_id=1, source_target_pairs={{0,1},{1,0},{2,3},{3,2},{4,5},{5,4},{6,7},{7,6},{8,9},{9,8},{10,11... | collective-permute-start | bytes 2015240 | tf_op jit(solution)/shard_map/ppermute | solution.py:213
  52.4 3.5 %collective-permute-start.13 = (bf16[328,1024]{1,0:T(8,128)(2,1)S(1)}, bf16[328,1024]{1,0:T(8,128)(2,1)S(1)}, u32[]{:S(2)}, u32[]{:S(2)}) collective-permute-start(bf16[328,1024]{1,0:T(8,128)(2,1)S(1)} %get-tuple-element.36.own_ref), channel_id=1, source_target_pairs={{0,2},{1,15},{2,4},{3,1},{4,6},{5,3},{6,8},{7,5},{8,10},{9,7},{10,... | collective-permute-start | bytes 2015240 | tf_op jit(solution)/shard_map/ppermute | solution.py:213
  55.9 8.2 %collective-permute-done.11.a_ref = bf16[328,1024]{1,0:T(8,128)(2,1)S(1)} collective-permute-done((bf16[328,1024]{1,0:T(8,128)(2,1)S(1)}, bf16[328,1024]{1,0:T(8,128)(2,1)S(1)}, u32[]{:S(2)}, u32[]{:S(2)}) %collective-permute-start.11) | collective-permute-done | bytes 671776 | tf_op jit(solution)/shard_map/ppermute | solution.py:213
  64.1 2.4 %collective-permute-start.16 = (bf16[328,1024]{1,0:T(8,128)(2,1)S(1)}, bf16[328,1024]{1,0:T(8,128)(2,1)S(1)}, u32[]{:S(2)}, u32[]{:S(2)}) collective-permute-start(bf16[328,1024]{1,0:T(8,128)(2,1)S(1)} %collective-permute-done.11.a_ref), channel_id=1, source_target_pairs={{0,14},{1,3},{2,0},{3,5},{4,2},{5,7},{6,4},{7,9},{8,6},{9,11},{10,... | collective-permute-start | bytes 2015240 | tf_op jit(solution)/shard_map/ppermute | solution.py:213
  66.5 0.0 collective-permute-done.12.twin_ref
  66.5 1.9 %collective-permute-start.15 = (bf16[328,1024]{1,0:T(8,128)(2,1)S(1)}, bf16[328,1024]{1,0:T(8,128)(2,1)S(1)}, u32[]{:S(2)}, u32[]{:S(2)}) collective-permute-start(bf16[328,1024]{1,0:T(8,128)(2,1)S(1)} %collective-permute-done.11.a_ref), channel_id=1, source_target_pairs={{0,1},{1,0},{2,3},{3,2},{4,5},{5,4},{6,7},{7,6},{8,9},{9,8},{10,11... | collective-permute-start | bytes 2015240 | tf_op jit(solution)/shard_map/ppermute | solution.py:213
  68.4 1.7 %collective-permute-done.13.b_ref = bf16[328,1024]{1,0:T(8,128)(2,1)S(1)} collective-permute-done((bf16[328,1024]{1,0:T(8,128)(2,1)S(1)}, bf16[328,1024]{1,0:T(8,128)(2,1)S(1)}, u32[]{:S(2)}, u32[]{:S(2)}) %collective-permute-start.13) | collective-permute-done | bytes 671776 | tf_op jit(solution)/shard_map/ppermute | solution.py:213
  70.1 1.9 %collective-permute-start.14 = (bf16[328,1024]{1,0:T(8,128)(2,1)S(1)}, bf16[328,1024]{1,0:T(8,128)(2,1)S(1)}, u32[]{:S(2)}, u32[]{:S(2)}) collective-permute-start(bf16[328,1024]{1,0:T(8,128)(2,1)S(1)} %collective-permute-done.13.b_ref), channel_id=1, source_target_pairs={{0,1},{1,0},{2,3},{3,2},{4,5},{5,4},{6,7},{7,6},{8,9},{9,8},{10,11... | collective-permute-start | bytes 2015240 | tf_op jit(solution)/shard_map/ppermute | solution.py:213
  72.1 2.2 %collective-permute-start.19 = (bf16[328,1024]{1,0:T(8,128)(2,1)S(1)}, bf16[328,1024]{1,0:T(8,128)(2,1)S(1)}, u32[]{:S(2)}, u32[]{:S(2)}) collective-permute-start(bf16[328,1024]{1,0:T(8,128)(2,1)S(1)} %collective-permute-done.13.b_ref), channel_id=1, source_target_pairs={{0,2},{1,15},{2,4},{3,1},{4,6},{5,3},{6,8},{7,5},{8,10},{9,7},{10,... | collective-permute-start | bytes 2015240 | tf_op jit(solution)/shard_map/ppermute | solution.py:213
  74.3 2.4 %collective-permute-done.16.a2_ref = bf16[328,1024]{1,0:T(8,128)(2,1)S(1)} collective-permute-done((bf16[328,1024]{1,0:T(8,128)(2,1)S(1)}, bf16[328,1024]{1,0:T(8,128)(2,1)S(1)}, u32[]{:S(2)}, u32[]{:S(2)}) %collective-permute-start.16) | collective-permute-done | bytes 671776 | tf_op jit(solution)/shard_map/ppermute | solution.py:213
  76.7 2.9 %collective-permute-start.18 = (bf16[168,1024]{1,0:T(8,128)(2,1)S(1)}, bf16[168,1024]{1,0:T(8,128)(2,1)S(1)}, u32[]{:S(2)}, u32[]{:S(2)}) collective-permute-start(bf16[168,1024]{1,0:T(8,128)(2,1)S(1)} %slice.21), channel_id=1, source_target_pairs={{0,1},{1,0},{2,3},{3,2},{4,5},{5,4},{6,7},{7,6},{8,9},{9,8},{10,11... | collective-permute-start | bytes 1032200 | tf_op jit(solution)/shard_map/ppermute | solution.py:213
  79.7 1.9 %collective-permute-start.17 = (bf16[160,1024]{1,0:T(8,128)(2,1)S(1)}, bf16[160,1024]{1,0:T(8,128)(2,1)S(1)}, u32[]{:S(2)}, u32[]{:S(2)}) collective-permute-start(bf16[160,1024]{1,0:T(8,128)(2,1)S(1)} %slice.20), channel_id=1, source_target_pairs={{0,1},{1,0},{2,3},{3,2},{4,5},{5,4},{6,7},{7,6},{8,9},{9,8},{10,11... | collective-permute-start | bytes 983048 | tf_op jit(solution)/shard_map/ppermute | solution.py:213
  81.6 0.0 collective-permute-done.15.b_twin_ref
  81.6 1.8 %shard_map.33.a2_best = f32[1,320]{1,0:T(1,128)S(1)} custom-call(bf16[328,1024]{1,0:T(8,128)(2,1)S(1)} %collective-permute-done.16.a2_ref, bf16[328,1024]{1,0:T(8,128)(2,1)S(1)} %get-tuple-element.36.own_ref, bf16[328,1024]{1,0:T(8,128)(2,1)S(1)} %collective-permute-done.12.twin_ref, bf16[328,1024]{1,0:T(8,128)(2,1)S(1)} %collective-permute-done.13.b_ref, ...), custom_call_target="tpu_custom_call" | custom-call | flops 943718400 | bytes 3358720 | tf_op jit(solution)/shard_map/pallas_call | solution.py:227
  83.5 0.0 collective-permute-done.18.twin_1
  83.5 0.6 shard_map.34.seen_ref
  84.1 7.9 %collective-permute-start.20 = (f32[1,384]{1,0:T(1,128)S(1)}, f32[1,384]{1,0:T(1,128)S(1)}, u32[]{:S(2)}, u32[]{:S(2)}) collective-permute-start(f32[1,384]{1,0:T(1,128)S(1)} %shard_map.34.seen_ref), channel_id=1, source_target_pairs={{0,4},{1,13},{2,6},{3,15},{4,8},{5,1},{6,10},{7,3},{8,12},{9,5},{1... | collective-permute-start | bytes 4616 | tf_op jit(solution)/shard_map/ppermute | solution.py:213
  92.0 2.2 %shard_map.35.seen_ref = f32[1,384]{1,0:T(1,128)S(1)} custom-call(f32[1,384]{1,0:T(1,128)S(1)} %shard_map.34.seen_ref, bf16[328,1024]{1,0:T(8,128)(2,1)S(1)} %collective-permute-done.19.b2_ref, bf16[328,1024]{1,0:T(8,128)(2,1)S(1)} %get-tuple-element.36.own_ref, bf16[328,1024]{1,0:T(8,128)(2,1)S(1)} %collective-permute-done.12.twin_ref, ...), custom_call_target="tpu_custom_call" | custom-call | flops 1179648000 | bytes 4030464 | tf_op jit(solution)/shard_map/pallas_call | solution.py:233
  94.3 1.9 %collective-permute-start.21 = (f32[1,384]{1,0:T(1,128)S(1)}, f32[1,384]{1,0:T(1,128)S(1)}, u32[]{:S(2)}, u32[]{:S(2)}) collective-permute-start(f32[1,384]{1,0:T(1,128)S(1)} %shard_map.35.seen_ref), channel_id=1, source_target_pairs={{0,12},{1,5},{2,14},{3,7},{4,0},{5,9},{6,2},{7,11},{8,4},{9,13},{1... | collective-permute-start | bytes 4616 | tf_op jit(solution)/shard_map/ppermute | solution.py:213
  96.2 2.7 %shard_map.32 = (f32[1,320]{1,0:T(1,128)S(1)}, s32[512,128]{1,0:T(8,128)S(1)}) custom-call(bf16[328,1024]{1,0:T(8,128)(2,1)S(1)} %get-tuple-element.36.own_ref, bf16[328,1024]{1,0:T(8,128)(2,1)S(1)} %collective-permute-done.12.twin_ref, bf16[328,1024]{1,0:T(8,128)(2,1)S(1)} %collective-permute-done.11.a_ref, ...), custom_call_target="tpu_custom_call" | custom-call | flops 1415577600 | bytes 4030464 | tf_op jit(solution)/shard_map/pallas_call | solution.py:236
  98.9 1.8 %collective-permute-done.21.told_b = f32[1,384]{1,0:T(1,128)S(1)} collective-permute-done((f32[1,384]{1,0:T(1,128)S(1)}, f32[1,384]{1,0:T(1,128)S(1)}, u32[]{:S(2)}, u32[]{:S(2)}) %collective-permute-start.21) | collective-permute-done | bytes 1568 | tf_op jit(solution)/shard_map/ppermute | solution.py:213
  100.7 0.8 shard_map.36
  101.5 3.8 %all-to-all-start.2 = ((f32[32,1,128]{2,1,0:T(1,128)}), f32[32,1,128]{2,1,0:T(1,128)S(1)}, u32[]{:S(2)}, u32[]{:S(2)}) async-start(f32[32,1,128]{2,1,0:T(1,128)} %bitcast.9), calls=%async_computation.2 | async-start | bytes 32768 | tf_op jit(solution)/shard_map/all_to_all | solution.py:252
  105.3 9.8 %all-to-all-done.2 = f32[32,1,128]{2,1,0:T(1,128)S(1)} async-done(((f32[32,1,128]{2,1,0:T(1,128)}), f32[32,1,128]{2,1,0:T(1,128)S(1)}, u32[]{:S(2)}, u32[]{:S(2)}) %all-to-all-start.2) | async-done | bytes 16416 | tf_op jit(solution)/shard_map/all_to_all | solution.py:252
  115.1 0.8 shard_map.37
  115.9 0.2 conditional.1
  (8 shorter events, 0.1 us)
Async XLA Ops:
  0.0 1.0 copy-start
  1.0 0.7 copy-start.1
  48.1 16.0 %collective-permute-start.11 = (bf16[328,1024]{1,0:T(8,128)(2,1)S(1)}, bf16[328,1024]{1,0:T(8,128)(2,1)S(1)}, u32[]{:S(2)}, u32[]{:S(2)}) collective-permute-start(bf16[328,1024]{1,0:T(8,128)(2,1)S(1)} %get-tuple-element.36.own_ref), channel_id=1, source_target_pairs={{0,14},{1,3},{2,0},{3,5},{4,2},{5,7},{6,4},{7,9},{8,6},{9,11},{10,... | collective-permute-start | bytes 2015240 | tf_op jit(solution)/shard_map/ppermute | solution.py:213
  50.5 16.0 %collective-permute-start.12 = (bf16[328,1024]{1,0:T(8,128)(2,1)S(1)}, bf16[328,1024]{1,0:T(8,128)(2,1)S(1)}, u32[]{:S(2)}, u32[]{:S(2)}) collective-permute-start(bf16[328,1024]{1,0:T(8,128)(2,1)S(1)} %get-tuple-element.36.own_ref), channel_id=1, source_target_pairs={{0,1},{1,0},{2,3},{3,2},{4,5},{5,4},{6,7},{7,6},{8,9},{9,8},{10,11... | collective-permute-start | bytes 2015240 | tf_op jit(solution)/shard_map/ppermute | solution.py:213
  52.4 17.8 %collective-permute-start.13 = (bf16[328,1024]{1,0:T(8,128)(2,1)S(1)}, bf16[328,1024]{1,0:T(8,128)(2,1)S(1)}, u32[]{:S(2)}, u32[]{:S(2)}) collective-permute-start(bf16[328,1024]{1,0:T(8,128)(2,1)S(1)} %get-tuple-element.36.own_ref), channel_id=1, source_target_pairs={{0,2},{1,15},{2,4},{3,1},{4,6},{5,3},{6,8},{7,5},{8,10},{9,7},{10,... | collective-permute-start | bytes 2015240 | tf_op jit(solution)/shard_map/ppermute | solution.py:213
  64.1 12.6 %collective-permute-start.16 = (bf16[328,1024]{1,0:T(8,128)(2,1)S(1)}, bf16[328,1024]{1,0:T(8,128)(2,1)S(1)}, u32[]{:S(2)}, u32[]{:S(2)}) collective-permute-start(bf16[328,1024]{1,0:T(8,128)(2,1)S(1)} %collective-permute-done.11.a_ref), channel_id=1, source_target_pairs={{0,14},{1,3},{2,0},{3,5},{4,2},{5,7},{6,4},{7,9},{8,6},{9,11},{10,... | collective-permute-start | bytes 2015240 | tf_op jit(solution)/shard_map/ppermute | solution.py:213
  66.5 15.1 %collective-permute-start.15 = (bf16[328,1024]{1,0:T(8,128)(2,1)S(1)}, bf16[328,1024]{1,0:T(8,128)(2,1)S(1)}, u32[]{:S(2)}, u32[]{:S(2)}) collective-permute-start(bf16[328,1024]{1,0:T(8,128)(2,1)S(1)} %collective-permute-done.11.a_ref), channel_id=1, source_target_pairs={{0,1},{1,0},{2,3},{3,2},{4,5},{5,4},{6,7},{7,6},{8,9},{9,8},{10,11... | collective-permute-start | bytes 2015240 | tf_op jit(solution)/shard_map/ppermute | solution.py:213
  70.1 21.9 %collective-permute-start.14 = (bf16[328,1024]{1,0:T(8,128)(2,1)S(1)}, bf16[328,1024]{1,0:T(8,128)(2,1)S(1)}, u32[]{:S(2)}, u32[]{:S(2)}) collective-permute-start(bf16[328,1024]{1,0:T(8,128)(2,1)S(1)} %collective-permute-done.13.b_ref), channel_id=1, source_target_pairs={{0,1},{1,0},{2,3},{3,2},{4,5},{5,4},{6,7},{7,6},{8,9},{9,8},{10,11... | collective-permute-start | bytes 2015240 | tf_op jit(solution)/shard_map/ppermute | solution.py:213
  72.1 20.0 %collective-permute-start.19 = (bf16[328,1024]{1,0:T(8,128)(2,1)S(1)}, bf16[328,1024]{1,0:T(8,128)(2,1)S(1)}, u32[]{:S(2)}, u32[]{:S(2)}) collective-permute-start(bf16[328,1024]{1,0:T(8,128)(2,1)S(1)} %collective-permute-done.13.b_ref), channel_id=1, source_target_pairs={{0,2},{1,15},{2,4},{3,1},{4,6},{5,3},{6,8},{7,5},{8,10},{9,7},{10,... | collective-permute-start | bytes 2015240 | tf_op jit(solution)/shard_map/ppermute | solution.py:213
  76.7 6.7 %collective-permute-start.18 = (bf16[168,1024]{1,0:T(8,128)(2,1)S(1)}, bf16[168,1024]{1,0:T(8,128)(2,1)S(1)}, u32[]{:S(2)}, u32[]{:S(2)}) collective-permute-start(bf16[168,1024]{1,0:T(8,128)(2,1)S(1)} %slice.21), channel_id=1, source_target_pairs={{0,1},{1,0},{2,3},{3,2},{4,5},{5,4},{6,7},{7,6},{8,9},{9,8},{10,11... | collective-permute-start | bytes 1032200 | tf_op jit(solution)/shard_map/ppermute | solution.py:213
  79.7 3.8 %collective-permute-start.17 = (bf16[160,1024]{1,0:T(8,128)(2,1)S(1)}, bf16[160,1024]{1,0:T(8,128)(2,1)S(1)}, u32[]{:S(2)}, u32[]{:S(2)}) collective-permute-start(bf16[160,1024]{1,0:T(8,128)(2,1)S(1)} %slice.20), channel_id=1, source_target_pairs={{0,1},{1,0},{2,3},{3,2},{4,5},{5,4},{6,7},{7,6},{8,9},{9,8},{10,11... | collective-permute-start | bytes 983048 | tf_op jit(solution)/shard_map/ppermute | solution.py:213
  84.1 16.6 %collective-permute-start.20 = (f32[1,384]{1,0:T(1,128)S(1)}, f32[1,384]{1,0:T(1,128)S(1)}, u32[]{:S(2)}, u32[]{:S(2)}) collective-permute-start(f32[1,384]{1,0:T(1,128)S(1)} %shard_map.34.seen_ref), channel_id=1, source_target_pairs={{0,4},{1,13},{2,6},{3,15},{4,8},{5,1},{6,10},{7,3},{8,12},{9,5},{1... | collective-permute-start | bytes 4616 | tf_op jit(solution)/shard_map/ppermute | solution.py:213
  94.3 6.4 %collective-permute-start.21 = (f32[1,384]{1,0:T(1,128)S(1)}, f32[1,384]{1,0:T(1,128)S(1)}, u32[]{:S(2)}, u32[]{:S(2)}) collective-permute-start(f32[1,384]{1,0:T(1,128)S(1)} %shard_map.35.seen_ref), channel_id=1, source_target_pairs={{0,12},{1,5},{2,14},{3,7},{4,0},{5,9},{6,2},{7,11},{8,4},{9,13},{1... | collective-permute-start | bytes 4616 | tf_op jit(solution)/shard_map/ppermute | solution.py:213
  101.5 13.6 %all-to-all-start.2 = ((f32[32,1,128]{2,1,0:T(1,128)}), f32[32,1,128]{2,1,0:T(1,128)S(1)}, u32[]{:S(2)}, u32[]{:S(2)}) async-start(f32[32,1,128]{2,1,0:T(1,128)} %bitcast.9), calls=%async_computation.2 | async-start | bytes 32768 | tf_op jit(solution)/shard_map/all_to_all | solution.py:252
